TPU v7x, 512 devices: a whole 4x4x16 slice. The times are simulated.
512 devices in a mesh: seq: 64 (over x, y, z_hi, core), tp: 8 (over z_lo).
Axes of the slice: x: 4, y: 4, z: 16 (z_hi: 2, z_lo: 8; z = z_hi * 8 + z_lo), core: 2. Of those that a mesh axis runs over, the one named last changes fastest.
Arguments:
- queries: bfloat16 [16384, 3072], P(('seq', 'tp')), may hold values from -6 to 6
- keys: bfloat16 [16384, 3072], P(('seq', 'tp')), may hold values from -6 to 6
- values: bfloat16 [16384, 3072], P(('seq', 'tp')), may hold values from -6 to 6
- out_grad: bfloat16 [16384, 3072], P(('seq', 'tp')), may hold values from -6 to 6
- tile_image: int32 [128], replicated, may hold values from 0 to 63, never falling along the last dimension, each value on 1 to 3 neighbouring positions
- pad_count: int32 [64], replicated, may hold values from 0 to 126
Outputs:
- attended: bfloat16 [16384, 3072], P('seq', 'tp')
- query_grad: bfloat16 [16384, 3072], P('seq', 'tp')
- key_grad: bfloat16 [16384, 3072], P('seq', 'tp')
- value_grad: bfloat16 [16384, 3072], P('seq', 'tp')
Inputs may be any that keep to these rules, and one draw needn't show every extreme that they name: `tile_image`: never falls along the pack; every image number owns 1 to 3 consecutive tiles, and some image owns exactly 3.
All inputs are finite; a program needn't handle non-finite values.
Results may differ from a plain program's by a relative error of at most 0.03.
Values may be sent and summed in bfloat16 or wider, within the bound.
No kernel may reach another device: no remote copies, remote signals or barrier semaphores. Data moves between devices by JAX's collectives and lax.ppermute only.
A program may use at most 64 MiB of HBM per device.

v0:
```python
import jax
import jax.numpy as jnp
from jax import lax
from jax.sharding import PartitionSpec as P

HEAD_DIM = 128
TILE = 128


masked_score = -1e30


def shifted(value, axis, steps):
    count = lax.axis_size(axis)
    leading, last = (max(0, -steps), min(count, count - steps))
    return lax.ppermute(value, axis, [(source, source + steps) for source in range(leading, last)])


def tile_limits(tile_image, pad_count):
    image_index = jnp.arange(pad_count.shape[0], dtype=jnp.int32)
    stop_tiles = jnp.sum((tile_image[None, :] <= image_index[:, None]).astype(jnp.int32), axis=1)
    end_tokens = stop_tiles * TILE - pad_count
    return jnp.sum(
        jnp.where(tile_image[:, None] == image_index[None, :], end_tokens[None, :], 0), axis=1
    )


def pair_mask(query_image, query_valid, key_image, key_valid):
    return (query_image[:, None] == key_image[None, :]) & query_valid[:, None] & key_valid[None, :]


def body(queries, keys, values, out_grad, tile_image, pad_count):
    query_rows, key_rows, value_rows, grad_rows = (
        lax.all_to_all(queries, "tp", split_axis=1, concat_axis=0, tiled=True),
        lax.all_to_all(keys, "tp", split_axis=1, concat_axis=0, tiled=True),
        lax.all_to_all(values, "tp", split_axis=1, concat_axis=0, tiled=True),
        lax.all_to_all(out_grad, "tp", split_axis=1, concat_axis=0, tiled=True),
    )
    row_count, lane_count = query_rows.shape
    head_count = lane_count // HEAD_DIM
    scaling = HEAD_DIM ** (-0.5)
    shard_index = lax.axis_index("seq")
    shard_total = lax.axis_size("seq")
    limits = tile_limits(tile_image, pad_count)
    tile_count = row_count // TILE

    def layout(offset):
        neighbor = shard_index + offset
        inside = (neighbor >= 0) & (neighbor < shard_total)
        clamped = jnp.clip(neighbor, 0, shard_total - 1)
        first_tile = clamped * tile_count
        block_image = jnp.repeat(lax.dynamic_slice_in_dim(tile_image, first_tile, tile_count), TILE)
        block_limit = jnp.repeat(lax.dynamic_slice_in_dim(limits, first_tile, tile_count), TILE)
        positions = first_tile * TILE + jnp.arange(row_count, dtype=jnp.int32)
        return (block_image, (positions < block_limit) & inside)

    def split_heads(array):
        return array.reshape(row_count, head_count, HEAD_DIM)

    own_image, own_valid = layout(0)
    own_queries = split_heads(query_rows)
    own_grad = split_heads(grad_rows)
    own_keys = split_heads(key_rows)
    own_values = split_heads(value_rows)
    blocks = [(0, own_keys, own_values)]
    distance = 1
    from_lower = shifted((key_rows, value_rows), "seq", distance)
    from_upper = shifted((key_rows, value_rows), "seq", -distance)
    blocks.append((-distance, split_heads(from_lower[0]), split_heads(from_lower[1])))
    blocks.append((distance, split_heads(from_upper[0]), split_heads(from_upper[1])))
    block_masks = []
    for block_index in range(len(blocks)):
        block_image, block_valid = layout(blocks[block_index][0])
        block_masks.append(pair_mask(own_image, own_valid, block_image, block_valid))

    def scores_of(query3, key3, allowed):
        raw_scores = jnp.einsum("qhd,khd->hqk", query3, key3, preferred_element_type=jnp.float32)
        return jnp.where(allowed[None], raw_scores * scaling, masked_score)

    def weights_of(query3, key3, allowed, row_total):
        scores = scores_of(query3, key3, allowed)
        return jnp.where(allowed[None], jnp.exp(scores - row_total[:, :, None]), 0.0)

    stat_shape = (head_count, row_count)
    zero_rows = jnp.zeros((row_count, head_count, HEAD_DIM), jnp.float32)
    row_top = jnp.full(stat_shape, masked_score, jnp.float32)
    row_total = jnp.zeros(stat_shape, jnp.float32)
    for block_index in range(len(blocks)):
        allowed = block_masks[block_index]
        first_scores = scores_of(own_queries, blocks[block_index][1], allowed)
        block_top = jnp.max(first_scores, axis=2)
        block_top, block_total = (
            block_top,
            jnp.sum(jnp.exp(first_scores - block_top[:, :, None]), axis=2),
        )
        new_top = jnp.maximum(row_top, block_top)
        row_total = row_total * jnp.exp(row_top - new_top) + block_total * jnp.exp(
            block_top - new_top
        )
        row_top = new_top
    log_total = jnp.where(
        own_valid[None], row_top + jnp.log(jnp.where(own_valid[None], row_total, 1.0)), 0.0
    )
    attended_sum = zero_rows
    for block_index in range(len(blocks)):
        allowed = block_masks[block_index]
        second_weights = weights_of(own_queries, blocks[block_index][1], allowed, log_total)
        attended_sum = attended_sum + jnp.einsum(
            "hqk,khd->qhd",
            second_weights.astype(jnp.bfloat16),
            blocks[block_index][2],
            preferred_element_type=jnp.float32,
        )
    attended = attended_sum.astype(jnp.bfloat16)
    grad_dot = jnp.einsum("qhd,qhd->hq", own_grad, attended, preferred_element_type=jnp.float32)

    def pair_grads(query3, grad3, query_total, query_dot, key3, value3, allowed):
        weights = weights_of(query3, key3, allowed, query_total)
        value_score = jnp.einsum("qhd,khd->hqk", grad3, value3, preferred_element_type=jnp.float32)
        score_grad = (weights * (value_score - query_dot[:, :, None])).astype(jnp.bfloat16)
        return (weights.astype(jnp.bfloat16), score_grad)

    def full_terms(operands):
        key3, value3, allowed = operands
        weight_half, score_grad = pair_grads(
            own_queries, own_grad, log_total, grad_dot, key3, value3, allowed
        )
        query_part = jnp.einsum(
            "hqk,khd->qhd", score_grad, key3, preferred_element_type=jnp.float32
        )
        key_part = jnp.einsum(
            "hqk,qhd->khd", score_grad, own_queries, preferred_element_type=jnp.float32
        )
        value_part = jnp.einsum(
            "hqk,qhd->khd", weight_half, own_grad, preferred_element_type=jnp.float32
        )
        return (query_part, key_part, value_part)

    query_sum, key_sum, value_sum = full_terms((own_keys, own_values, block_masks[0]))
    distance = 1
    lower_index = 2 * distance - 1
    upper_index = 2 * distance
    lower_query, lower_key, lower_value = full_terms(
        (blocks[lower_index][1], blocks[lower_index][2], block_masks[lower_index])
    )
    upper_query, upper_key, upper_value = full_terms(
        (blocks[upper_index][1], blocks[upper_index][2], block_masks[upper_index])
    )
    query_sum = query_sum + lower_query + upper_query
    back_lower = (
        shifted(lower_key.astype(jnp.bfloat16), "seq", -distance).astype(lower_key.dtype),
        shifted(lower_value.astype(jnp.bfloat16), "seq", -distance).astype(lower_value.dtype),
    )
    back_upper = (
        shifted(upper_key.astype(jnp.bfloat16), "seq", distance).astype(upper_key.dtype),
        shifted(upper_value.astype(jnp.bfloat16), "seq", distance).astype(upper_value.dtype),
    )
    key_sum = key_sum + back_lower[0] + back_upper[0]
    value_sum = value_sum + back_lower[1] + back_upper[1]
    attended_out = attended.reshape(row_count, lane_count)
    query_grad = (query_sum * scaling).astype(jnp.bfloat16).reshape(row_count, lane_count)
    key_grad = (key_sum * scaling).astype(jnp.bfloat16).reshape(row_count, lane_count)
    value_grad = value_sum.astype(jnp.bfloat16).reshape(row_count, lane_count)
    return (attended_out, query_grad, key_grad, value_grad)


def solution(mesh):
    in_specs = (
        P(("seq", "tp"), None),
        P(("seq", "tp"), None),
        P(("seq", "tp"), None),
        P(("seq", "tp"), None),
        P(),
        P(),
    )
    out_specs = (P("seq", "tp"), P("seq", "tp"), P("seq", "tp"), P("seq", "tp"))
    return jax.shard_map(body, mesh=mesh, in_specs=in_specs, out_specs=out_specs, check_vma=False)
```

profile of v0, /device:TPU:24, one launch (start us, length us, event | category | flops | bytes accessed | tf_op | source)
XLA Modules:
  0.0 191.9 jit_solution(8937197855346334239)
XLA Ops:
  0.6 1.6 copy.299
  2.3 12.7 %all-to-all-start.2 = ((bf16[32,8,384]{2,0,1:T(8,128)(2,1)}), bf16[32,8,384]{2,0,1:T(8,128)(2,1)}, u32[]{:S(2)}, u32[]{:S(2)}) async-start(bf16[32,8,384]{2,0,1:T(8,128)(2,1)} %bitcast.83), calls=%async_computation.2 | async-start | bytes 393216 | tf_op jit(solution)/shard_map/all_to_all | solution.py:36
  14.9 0.7 copy.297
  15.6 13.3 %all-to-all-done.2 = bf16[32,8,384]{2,0,1:T(8,128)(2,1)} async-done(((bf16[32,8,384]{2,0,1:T(8,128)(2,1)}), bf16[32,8,384]{2,0,1:T(8,128)(2,1)}, u32[]{:S(2)}, u32[]{:S(2)}) %all-to-all-start.2) | async-done | bytes 196640 | tf_op jit(solution)/shard_map/all_to_all | solution.py:36
  28.9 5.2 %all-to-all-start.1 = ((bf16[32,8,384]{2,0,1:T(8,128)(2,1)}), bf16[32,8,384]{2,0,1:T(8,128)(2,1)S(1)}, u32[]{:S(2)}, u32[]{:S(2)}) async-start(bf16[32,8,384]{2,0,1:T(8,128)(2,1)} %bitcast.81), calls=%async_computation.1 | async-start | bytes 393216 | tf_op jit(solution)/shard_map/all_to_all | solution.py:35
  34.3 0.7 copy.298
  35.0 0.7 copy-done.22
  35.9 12.2 %all-to-all-done.1 = bf16[32,8,384]{2,0,1:T(8,128)(2,1)S(1)} async-done(((bf16[32,8,384]{2,0,1:T(8,128)(2,1)}), bf16[32,8,384]{2,0,1:T(8,128)(2,1)S(1)}, u32[]{:S(2)}, u32[]{:S(2)}) %all-to-all-start.1) | async-done | bytes 196640 | tf_op jit(solution)/shard_map/all_to_all | solution.py:35
  48.0 5.2 %all-to-all-start = ((bf16[32,8,384]{2,0,1:T(8,128)(2,1)}), bf16[32,8,384]{2,0,1:T(8,128)(2,1)S(1)}, u32[]{:S(2)}, u32[]{:S(2)}) async-start(bf16[32,8,384]{2,0,1:T(8,128)(2,1)} %bitcast.82), calls=%async_computation | async-start | bytes 393216 | tf_op jit(solution)/shard_map/all_to_all | solution.py:34
  53.3 0.7 copy.296
  54.2 12.9 %all-to-all-done = bf16[32,8,384]{2,0,1:T(8,128)(2,1)S(1)} async-done(((bf16[32,8,384]{2,0,1:T(8,128)(2,1)}), bf16[32,8,384]{2,0,1:T(8,128)(2,1)S(1)}, u32[]{:S(2)}, u32[]{:S(2)}) %all-to-all-start) | async-done | bytes 196640 | tf_op jit(solution)/shard_map/all_to_all | solution.py:34
  67.2 5.1 %all-to-all-start.3 = ((bf16[32,8,384]{2,0,1:T(8,128)(2,1)}), bf16[32,8,384]{2,0,1:T(8,128)(2,1)S(1)}, u32[]{:S(2)}, u32[]{:S(2)}) async-start(bf16[32,8,384]{2,0,1:T(8,128)(2,1)} %bitcast.80), calls=%async_computation.3 | async-start | bytes 393216 | tf_op jit(solution)/shard_map/all_to_all | solution.py:37
  72.6 7.6 %collective-permute-start.1 = (bf16[256,384]{1,0:T(8,128)(2,1)S(1)}, bf16[256,384]{1,0:T(8,128)(2,1)S(1)}, u32[]{:S(2)}, u32[]{:S(2)}) collective-permute-start(bf16[256,384]{1,0:T(8,128)(2,1)S(1)} %bitcast.89), channel_id=1, source_target_pairs={{8,0},{16,8},{24,16},{32,24},{40,32},{48,40},{56,48},{64,56},{72,6... | collective-permute-start | bytes 589832 | tf_op jit(solution)/shard_map/ppermute | solution.py:16
  80.2 1.9 %collective-permute-start = (bf16[256,384]{1,0:T(8,128)(2,1)S(1)}, bf16[256,384]{1,0:T(8,128)(2,1)S(1)}, u32[]{:S(2)}, u32[]{:S(2)}) collective-permute-start(bf16[256,384]{1,0:T(8,128)(2,1)S(1)} %bitcast.90), channel_id=1, source_target_pairs={{0,8},{8,16},{16,24},{24,32},{32,40},{40,48},{48,56},{56,64},{64,7... | collective-permute-start | bytes 589832 | tf_op jit(solution)/shard_map/ppermute | solution.py:16
  82.1 6.3 %collective-permute-start.2 = (bf16[256,384]{1,0:T(8,128)(2,1)}, bf16[256,384]{1,0:T(8,128)(2,1)}, u32[]{:S(2)}, u32[]{:S(2)}) collective-permute-start(bf16[256,384]{1,0:T(8,128)(2,1)} %bitcast.15), channel_id=1, source_target_pairs={{0,8},{8,16},{16,24},{24,32},{32,40},{40,48},{48,56},{56,64},{64,7... | collective-permute-start | bytes 589832 | tf_op jit(solution)/shard_map/ppermute | solution.py:16
  88.4 8.9 %collective-permute-start.3 = (bf16[256,384]{1,0:T(8,128)(2,1)}, bf16[256,384]{1,0:T(8,128)(2,1)}, u32[]{:S(2)}, u32[]{:S(2)}) collective-permute-start(bf16[256,384]{1,0:T(8,128)(2,1)} %bitcast.15), channel_id=1, source_target_pairs={{8,0},{16,8},{24,16},{32,24},{40,32},{48,40},{56,48},{64,56},{72,6... | collective-permute-start | bytes 589832 | tf_op jit(solution)/shard_map/ppermute | solution.py:16
  97.7 0.6 copy-done
  98.6 1.0 reshape.369
  99.6 0.8 reshape.373
  100.7 0.3 fusion.66
  101.1 17.9 %collective-permute-done = bf16[256,384]{1,0:T(8,128)(2,1)S(1)} collective-permute-done((bf16[256,384]{1,0:T(8,128)(2,1)S(1)}, bf16[256,384]{1,0:T(8,128)(2,1)S(1)}, u32[]{:S(2)}, u32[]{:S(2)}) %collective-permute-start) | collective-permute-done | bytes 196640 | tf_op jit(solution)/shard_map/ppermute | solution.py:16
  119.2 0.3 fusion.68
  119.5 0.3 copy-done.2
  120.1 1.0 fusion.19
  121.1 4.6 %collective-permute-done.2 = bf16[256,384]{1,0:T(8,128)(2,1)} collective-permute-done((bf16[256,384]{1,0:T(8,128)(2,1)}, bf16[256,384]{1,0:T(8,128)(2,1)}, u32[]{:S(2)}, u32[]{:S(2)}) %collective-permute-start.2) | collective-permute-done | bytes 196640 | tf_op jit(solution)/shard_map/ppermute | solution.py:16
  125.7 1.1 copy.192
  126.8 1.3 convolution_add_fusion.3
  128.1 1.7 copy.194
  129.9 1.2 fusion.11
  131.3 2.0 %multiply_reduce_fusion = f32[3,256]{0,1:T(8,128)} fusion(f32[3,256,128]{2,0,1:T(4,128)S(1)} %copy.237, bf16[256,3,128]{2,1,0:T(4,128)(2,1)} %reshape.373), kind=kLoop, calls=%fused_computation.41 | loop fusion | flops 294144 | bytes 592896
  133.2 1.0 copy.238
  134.3 2.2 %fusion.6 = bf16[3,256,256]{1,2,0:T(8,128)(2,1)} fusion(f32[3,256,256]{1,2,0:T(8,128)S(1)} %get-tuple-element.36, f32[3,256]{1,0:T(4,128)S(1)} %copy.238, f32[3,256]{1,0:T(4,128)S(1)} %add_select_fusion, pred[256,256]{0,1:T(8,128)(4,1)S(1)} %copy-done.13, bf16[256,3,128]{2,1,0:T(4,128)(2,1)} %copy-done.8, bf16[256,3,128]{2,1,0:T(4,128)(2,1)} %reshape.373), kind=kOutput, calls=%fused_computation.12 | convolution fusion | flops 51314688 | bytes 1644544 | tf_op jit(solution)/shard_map/qhd,khd->hqk/dot_general | solution.py:119
  136.5 1.1 fusion.7
  137.6 0.4 fusion.8
  138.0 1.0 fusion.15
  139.0 0.8 copy.222
  139.9 1.3 fusion.69
  141.2 1.0 fusion.12
  142.4 1.0 fusion.13
  143.6 0.8 copy.223
  144.4 2.0 %collective-permute-start.5 = (bf16[256,3,128]{0,2,1:T(8,128)(2,1)}, bf16[256,3,128]{0,2,1:T(8,128)(2,1)S(1)}, u32[]{:S(2)}, u32[]{:S(2)}) collective-permute-start(bf16[256,3,128]{0,2,1:T(8,128)(2,1)} %fusion.13), channel_id=1, source_target_pairs={{0,8},{8,16},{16,24},{24,32},{32,40},{40,48},{48,56},{56,64},{64,7... | collective-permute-start | bytes 589832 | tf_op jit(solution)/shard_map/ppermute | solution.py:16
  146.5 13.3 %collective-permute-start.4 = (bf16[256,3,128]{0,2,1:T(8,128)(2,1)}, bf16[256,3,128]{0,2,1:T(8,128)(2,1)S(1)}, u32[]{:S(2)}, u32[]{:S(2)}) collective-permute-start(bf16[256,3,128]{0,2,1:T(8,128)(2,1)} %fusion.12), channel_id=1, source_target_pairs={{8,0},{16,8},{24,16},{32,24},{40,32},{48,40},{56,48},{64,56},{72,6... | collective-permute-start | bytes 589832 | tf_op jit(solution)/shard_map/ppermute | solution.py:16
  159.7 1.9 %collective-permute-start.7 = (bf16[256,3,128]{0,2,1:T(8,128)(2,1)}, bf16[256,3,128]{0,2,1:T(8,128)(2,1)S(1)}, u32[]{:S(2)}, u32[]{:S(2)}) collective-permute-start(bf16[256,3,128]{0,2,1:T(8,128)(2,1)} %fusion.15), channel_id=1, source_target_pairs={{0,8},{8,16},{16,24},{24,32},{32,40},{40,48},{48,56},{56,64},{64,7... | collective-permute-start | bytes 589832 | tf_op jit(solution)/shard_map/ppermute | solution.py:16
  162.0 13.2 %collective-permute-start.6 = (bf16[256,3,128]{0,2,1:T(8,128)(2,1)S(1)}, bf16[256,3,128]{0,2,1:T(8,128)(2,1)S(1)}, u32[]{:S(2)}, u32[]{:S(2)}) collective-permute-start(bf16[256,3,128]{0,2,1:T(8,128)(2,1)S(1)} %fusion.14), channel_id=1, source_target_pairs={{8,0},{16,8},{24,16},{32,24},{40,32},{48,40},{56,48},{64,56},{72,6... | collective-permute-start | bytes 589832 | tf_op jit(solution)/shard_map/ppermute | solution.py:16
  175.6 0.8 copy.224
  176.4 6.8 %collective-permute-done.7 = bf16[256,3,128]{0,2,1:T(8,128)(2,1)S(1)} collective-permute-done((bf16[256,3,128]{0,2,1:T(8,128)(2,1)}, bf16[256,3,128]{0,2,1:T(8,128)(2,1)S(1)}, u32[]{:S(2)}, u32[]{:S(2)}) %collective-permute-start.7) | collective-permute-done | bytes 196640 | tf_op jit(solution)/shard_map/ppermute | solution.py:16
  183.2 7.5 %collective-permute-done.6 = bf16[256,3,128]{0,2,1:T(8,128)(2,1)S(1)} collective-permute-done((bf16[256,3,128]{0,2,1:T(8,128)(2,1)S(1)}, bf16[256,3,128]{0,2,1:T(8,128)(2,1)S(1)}, u32[]{:S(2)}, u32[]{:S(2)}) %collective-permute-start.6) | collective-permute-done | bytes 196640 | tf_op jit(solution)/shard_map/ppermute | solution.py:16
  191.0 0.8 copy.225
  (75 shorter events, 4.1 us)
Async XLA Ops:
  2.3 12.7 %copy-start.18 = (bf16[32,3072]{1,0:T(8,128)(2,1)S(1)}, bf16[32,3072]{1,0:T(8,128)(2,1)}, u32[]{:S(2)}) copy-start(bf16[32,3072]{1,0:T(8,128)(2,1)} %param.7) | copy-start | bytes 589828
  2.3 26.7 %all-to-all-start.2 = ((bf16[32,8,384]{2,0,1:T(8,128)(2,1)}), bf16[32,8,384]{2,0,1:T(8,128)(2,1)}, u32[]{:S(2)}, u32[]{:S(2)}) async-start(bf16[32,8,384]{2,0,1:T(8,128)(2,1)} %bitcast.83), calls=%async_computation.2 | async-start | bytes 393216 | tf_op jit(solution)/shard_map/all_to_all | solution.py:36
  28.9 5.2 %copy-start.21 = (s32[128]{0:T(128)S(1)}, s32[128]{0:T(128)}, u32[]{:S(2)}) copy-start(s32[128]{0:T(128)} %param.10) | copy-start | bytes 1540
  28.9 5.3 %copy-start.19 = (bf16[32,3072]{1,0:T(8,128)(2,1)S(1)}, bf16[32,3072]{1,0:T(8,128)(2,1)}, u32[]{:S(2)}) copy-start(bf16[32,3072]{1,0:T(8,128)(2,1)} %param.6) | copy-start | bytes 589828
  28.9 19.1 %all-to-all-start.1 = ((bf16[32,8,384]{2,0,1:T(8,128)(2,1)}), bf16[32,8,384]{2,0,1:T(8,128)(2,1)S(1)}, u32[]{:S(2)}, u32[]{:S(2)}) async-start(bf16[32,8,384]{2,0,1:T(8,128)(2,1)} %bitcast.81), calls=%async_computation.1 | async-start | bytes 393216 | tf_op jit(solution)/shard_map/all_to_all | solution.py:35
  35.0 0.7 copy-start.22
  48.0 5.3 %copy-start.20 = (bf16[32,3072]{1,0:T(8,128)(2,1)S(1)}, bf16[32,3072]{1,0:T(8,128)(2,1)}, u32[]{:S(2)}) copy-start(bf16[32,3072]{1,0:T(8,128)(2,1)} %param.9) | copy-start | bytes 589828
  48.0 19.1 %all-to-all-start = ((bf16[32,8,384]{2,0,1:T(8,128)(2,1)}), bf16[32,8,384]{2,0,1:T(8,128)(2,1)S(1)}, u32[]{:S(2)}, u32[]{:S(2)}) async-start(bf16[32,8,384]{2,0,1:T(8,128)(2,1)} %bitcast.82), calls=%async_computation | async-start | bytes 393216 | tf_op jit(solution)/shard_map/all_to_all | solution.py:34
  67.2 32.4 %all-to-all-start.3 = ((bf16[32,8,384]{2,0,1:T(8,128)(2,1)}), bf16[32,8,384]{2,0,1:T(8,128)(2,1)S(1)}, u32[]{:S(2)}, u32[]{:S(2)}) async-start(bf16[32,8,384]{2,0,1:T(8,128)(2,1)} %bitcast.80), calls=%async_computation.3 | async-start | bytes 393216 | tf_op jit(solution)/shard_map/all_to_all | solution.py:37
  72.6 47.5 %copy-start.12 = (pred[256,256]{0,1:T(8,128)(4,1)}, pred[256,256]{0,1:T(8,128)(4,1)S(1)}, u32[]{:S(2)}) copy-start(pred[256,256]{0,1:T(8,128)(4,1)S(1)} %get-tuple-element.26) | copy-start | bytes 196612
  72.6 54.2 %copy-start.14 = (pred[256,256]{0,1:T(8,128)(4,1)}, pred[256,256]{0,1:T(8,128)(4,1)S(1)}, u32[]{:S(2)}) copy-start(pred[256,256]{0,1:T(8,128)(4,1)S(1)} %get-tuple-element.24) | copy-start | bytes 196612
  72.6 57.3 %copy-start.16 = (pred[256,256]{0,1:T(8,128)(4,1)}, pred[256,256]{0,1:T(8,128)(4,1)S(1)}, u32[]{:S(2)}) copy-start(pred[256,256]{0,1:T(8,128)(4,1)S(1)} %get-tuple-element.25) | copy-start | bytes 196612
  72.6 27.9 %collective-permute-start.1 = (bf16[256,384]{1,0:T(8,128)(2,1)S(1)}, bf16[256,384]{1,0:T(8,128)(2,1)S(1)}, u32[]{:S(2)}, u32[]{:S(2)}) collective-permute-start(bf16[256,384]{1,0:T(8,128)(2,1)S(1)} %bitcast.89), channel_id=1, source_target_pairs={{8,0},{16,8},{24,16},{32,24},{40,32},{48,40},{56,48},{64,56},{72,6... | collective-permute-start | bytes 589832 | tf_op jit(solution)/shard_map/ppermute | solution.py:16
  80.2 38.8 %collective-permute-start = (bf16[256,384]{1,0:T(8,128)(2,1)S(1)}, bf16[256,384]{1,0:T(8,128)(2,1)S(1)}, u32[]{:S(2)}, u32[]{:S(2)}) collective-permute-start(bf16[256,384]{1,0:T(8,128)(2,1)S(1)} %bitcast.90), channel_id=1, source_target_pairs={{0,8},{8,16},{16,24},{24,32},{32,40},{40,48},{48,56},{56,64},{64,7... | collective-permute-start | bytes 589832 | tf_op jit(solution)/shard_map/ppermute | solution.py:16
  82.1 43.6 %collective-permute-start.2 = (bf16[256,384]{1,0:T(8,128)(2,1)}, bf16[256,384]{1,0:T(8,128)(2,1)}, u32[]{:S(2)}, u32[]{:S(2)}) collective-permute-start(bf16[256,384]{1,0:T(8,128)(2,1)} %bitcast.15), channel_id=1, source_target_pairs={{0,8},{8,16},{16,24},{24,32},{32,40},{40,48},{48,56},{56,64},{64,7... | collective-permute-start | bytes 589832 | tf_op jit(solution)/shard_map/ppermute | solution.py:16
  88.4 39.7 %collective-permute-start.3 = (bf16[256,384]{1,0:T(8,128)(2,1)}, bf16[256,384]{1,0:T(8,128)(2,1)}, u32[]{:S(2)}, u32[]{:S(2)}) collective-permute-start(bf16[256,384]{1,0:T(8,128)(2,1)} %bitcast.15), channel_id=1, source_target_pairs={{8,0},{16,8},{24,16},{32,24},{40,32},{48,40},{56,48},{64,56},{72,6... | collective-permute-start | bytes 589832 | tf_op jit(solution)/shard_map/ppermute | solution.py:16
  97.6 0.7 copy-start
  99.6 20.5 %copy-start.8 = (bf16[256,3,128]{2,1,0:T(4,128)(2,1)}, bf16[256,3,128]{2,1,0:T(4,128)(2,1)S(1)}, u32[]{:S(2)}) copy-start(bf16[256,3,128]{2,1,0:T(4,128)(2,1)S(1)} %reshape.369) | copy-start | bytes 589828
  119.2 0.7 copy-start.2
  126.8 1.4 copy-start.9
  133.2 1.0 copy-start.13
  134.2 2.2 %copy-start.6 = (bf16[256,3,128]{2,1,0:T(4,128)(2,1)S(1)}, bf16[256,3,128]{2,1,0:T(4,128)(2,1)}, u32[]{:S(2)}) copy-start(bf16[256,3,128]{2,1,0:T(4,128)(2,1)} %reshape.373) | copy-start | bytes 589828
  134.3 2.2 %copy-start.10 = (bf16[256,384]{0,1:T(8,128)(2,1)S(1)}, bf16[256,384]{0,1:T(8,128)(2,1)}, u32[]{:S(2)}) copy-start(bf16[256,384]{0,1:T(8,128)(2,1)} %copy-done.9) | copy-start | bytes 589828
  134.3 2.2 %copy-start.15 = (pred[256,256]{0,1:T(8,128)(4,1)S(1)}, pred[256,256]{0,1:T(8,128)(4,1)}, u32[]{:S(2)}) copy-start(pred[256,256]{0,1:T(8,128)(4,1)} %copy-done.14) | copy-start | bytes 196612
  136.4 1.2 copy-start.11
  136.5 1.2 copy-start.17
  139.0 0.9 copy-start.1
  139.9 1.3 copy-start.4
  141.2 1.0 copy-start.3
  143.6 18.1 %copy-start.7 = (bf16[256,3,128]{2,1,0:T(4,128)(2,1)S(1)}, bf16[256,3,128]{2,1,0:T(4,128)(2,1)}, u32[]{:S(2)}) copy-start(bf16[256,3,128]{2,1,0:T(4,128)(2,1)} %reshape.373) | copy-start | bytes 589828
  144.4 30.8 %copy-start.5 = (bf16[3,256,256]{1,2,0:T(8,128)(2,1)S(1)}, bf16[3,256,256]{1,2,0:T(8,128)(2,1)}, u32[]{:S(2)}) copy-start(bf16[3,256,256]{1,2,0:T(8,128)(2,1)} %fusion.6) | copy-start | bytes 1179652
  144.4 30.8 %collective-permute-start.5 = (bf16[256,3,128]{0,2,1:T(8,128)(2,1)}, bf16[256,3,128]{0,2,1:T(8,128)(2,1)S(1)}, u32[]{:S(2)}, u32[]{:S(2)}) collective-permute-start(bf16[256,3,128]{0,2,1:T(8,128)(2,1)} %fusion.13), channel_id=1, source_target_pairs={{0,8},{8,16},{16,24},{24,32},{32,40},{40,48},{48,56},{56,64},{64,7... | collective-permute-start | bytes 589832 | tf_op jit(solution)/shard_map/ppermute | solution.py:16
  146.5 28.8 %collective-permute-start.4 = (bf16[256,3,128]{0,2,1:T(8,128)(2,1)}, bf16[256,3,128]{0,2,1:T(8,128)(2,1)S(1)}, u32[]{:S(2)}, u32[]{:S(2)}) collective-permute-start(bf16[256,3,128]{0,2,1:T(8,128)(2,1)} %fusion.12), channel_id=1, source_target_pairs={{8,0},{16,8},{24,16},{32,24},{40,32},{48,40},{56,48},{64,56},{72,6... | collective-permute-start | bytes 589832 | tf_op jit(solution)/shard_map/ppermute | solution.py:16
  159.7 23.5 %collective-permute-start.7 = (bf16[256,3,128]{0,2,1:T(8,128)(2,1)}, bf16[256,3,128]{0,2,1:T(8,128)(2,1)S(1)}, u32[]{:S(2)}, u32[]{:S(2)}) collective-permute-start(bf16[256,3,128]{0,2,1:T(8,128)(2,1)} %fusion.15), channel_id=1, source_target_pairs={{0,8},{8,16},{16,24},{24,32},{32,40},{40,48},{48,56},{56,64},{64,7... | collective-permute-start | bytes 589832 | tf_op jit(solution)/shard_map/ppermute | solution.py:16
  162.0 28.7 %collective-permute-start.6 = (bf16[256,3,128]{0,2,1:T(8,128)(2,1)S(1)}, bf16[256,3,128]{0,2,1:T(8,128)(2,1)S(1)}, u32[]{:S(2)}, u32[]{:S(2)}) collective-permute-start(bf16[256,3,128]{0,2,1:T(8,128)(2,1)S(1)} %fusion.14), channel_id=1, source_target_pairs={{8,0},{16,8},{24,16},{32,24},{40,32},{48,40},{56,48},{64,56},{72,6... | collective-permute-start | bytes 589832 | tf_op jit(solution)/shard_map/ppermute | solution.py:16
where the time goes:
time: 193 us; the launch traced here: 192 us
  starting transfers between devices  83.3 us (43%)
  waiting for transfers between devices  75.3 us (39%)
  local copies, waits for them, and re-layouts  15.4 us (8%)
  matrix products  13.8 us (7%)
  other arithmetic  3.07 us (2%)
    ppermute x8, starting transfers between devices, shifted(): lax.ppermute(value, axis, [(source, source + steps) for source in range(l...  55.2 us
    ppermute x8, waiting for transfers between devices, shifted(): lax.ppermute(value, axis, [(source, source + steps) for source in range(l...  36.9 us
    all_to_all x1, waiting for transfers between devices, body(): lax.all_to_all(values, 'tp', split_axis=1, concat_axis=0, tiled=True)  13.3 us
    all_to_all x1, waiting for transfers between devices, body(): lax.all_to_all(queries, 'tp', split_axis=1, concat_axis=0, tiled=True)  12.9 us
    all_to_all x1, starting transfers between devices, body(): lax.all_to_all(values, 'tp', split_axis=1, concat_axis=0, tiled=True)  12.7 us
    all_to_all x1, waiting for transfers between devices, body(): lax.all_to_all(keys, 'tp', split_axis=1, concat_axis=0, tiled=True)  12.2 us
    unnamed x51, local copies, waits for them, and re-layouts  5.24 us
    all_to_all x1, starting transfers between devices, body(): lax.all_to_all(keys, 'tp', split_axis=1, concat_axis=0, tiled=True)  5.2 us
  transfers between devices with their start and end apart: 12, of which 7 were waited for; matrix products, arithmetic and copies ran while one was open for 6% of the time, Pallas kernels for 0%

commit v1 on v0

v1 whole, which is shorter than its diff:
```python
import jax
import jax.numpy as jnp
from jax import lax
from jax.experimental import pallas as pl
from jax.experimental.pallas import tpu as pltpu
from jax.sharding import PartitionSpec as P

HEAD_DIM = 128
TILE = 128
WINDOW = 3
BF16 = jnp.bfloat16
F32 = jnp.float32


def image_ends(tile_image, pad_count):
    image_index = jnp.arange(pad_count.shape[0], dtype=jnp.int32)
    stop_tiles = jnp.sum((tile_image[None, :] <= image_index[:, None]).astype(jnp.int32), axis=1)
    return stop_tiles * TILE - pad_count


def tile_plan(tile_image, pad_count, seq_index, tile_count):
    ends = image_ends(tile_image, pad_count)
    tiles = jnp.arange(tile_image.shape[0], dtype=jnp.int32)
    images = jnp.arange(pad_count.shape[0], dtype=jnp.int32)
    plan = []
    for tile in range(tile_count):
        place = seq_index * tile_count + tile
        image = jnp.sum(jnp.where(tiles == place, tile_image, 0))
        first = jnp.sum((tile_image < image).astype(jnp.int32))
        end = jnp.sum(jnp.where(images == image, ends, 0))
        back = place - first
        plan += [tile_count + tile - back, back, end - first * TILE]
    return jnp.stack(plan).astype(jnp.int32)


def attention_kernel(
    plan_ref, near_ref, pair_ref, attended_ref, query_ref, key_ref, value_ref, rows, weight_buf, grad_buf, sems
):
    heads = attended_ref.shape[1] // HEAD_DIM
    tile_count = attended_ref.shape[0] // TILE
    near_chunks, pair_chunks = near_ref.shape[0], pair_ref.shape[0]
    chunk = near_ref.shape[2]
    per_tile = TILE // chunk
    scaling = HEAD_DIM ** (-0.5)
    near_at, pair_at = plan_ref[3 * tile_count], plan_ref[3 * tile_count + 1]
    copies = (
        pltpu.make_async_copy(pair_ref, rows.at[pl.ds(pair_at, pair_chunks)], sems.at[0]),
        pltpu.make_async_copy(near_ref, rows.at[pl.ds(near_at, near_chunks)], sems.at[1]),
    )
    for copy in copies:
        copy.start()
    for copy in copies:
        copy.wait()
    contract_last = (((1,), (1,)), ((), ()))
    contract_first = (((0,), (0,)), ((), ()))

    def dot(left, right, dims):
        return lax.dot_general(left, right, dims, preferred_element_type=F32)

    column = lax.broadcasted_iota(jnp.int32, (TILE, WINDOW * TILE), 1)
    row = lax.broadcasted_iota(jnp.int32, (TILE, 1), 0)
    for tile in range(tile_count):
        start, back, live = plan_ref[3 * tile], plan_ref[3 * tile + 1], plan_ref[3 * tile + 2]
        seen = column < live
        own = pl.ds(tile * TILE, TILE)
        own_window = pl.ds(pl.multiple_of(back * TILE, TILE), TILE)
        for head in range(heads):
            lanes = slice(head * HEAD_DIM, (head + 1) * HEAD_DIM)

            def part(index, first, count):
                block = rows[pl.ds(first * per_tile, count * per_tile), index, :, lanes]
                return block.reshape(count * TILE, HEAD_DIM)

            keys, values = part(1, start, WINDOW), part(2, start, WINDOW)
            for step in range(WINDOW):
                queries, grads = part(0, start + step, 1), part(3, start + step, 1)
                scores = jnp.where(seen, dot(queries, keys, contract_last) * scaling, -1e30)
                top = jnp.max(scores, axis=1, keepdims=True)
                raised = jnp.exp(scores - top)
                total = jnp.sum(raised, axis=1, keepdims=True)
                inverse = jnp.where(row + step * TILE < live, 1.0 / total, 0.0)
                weights = raised * inverse
                value_score = dot(grads, values, contract_last)
                grad_dot = jnp.sum(weights * value_score, axis=1, keepdims=True)
                score_grad = weights * (value_score - grad_dot)
                weight_buf[step * TILE : (step + 1) * TILE, :] = weights.astype(BF16)
                grad_buf[step * TILE : (step + 1) * TILE, :] = score_grad.astype(BF16)
            queries, grads = part(0, start, WINDOW), part(3, start, WINDOW)
            attended_ref[own, lanes] = jnp.dot(weight_buf[own_window, :], values, preferred_element_type=F32).astype(BF16)
            query_ref[own, lanes] = (jnp.dot(grad_buf[own_window, :], keys, preferred_element_type=F32) * scaling).astype(BF16)
            key_ref[own, lanes] = (dot(grad_buf[:, own_window], queries, contract_first) * scaling).astype(BF16)
            value_ref[own, lanes] = dot(weight_buf[:, own_window], grads, contract_first).astype(BF16)


def body(queries, keys, values, out_grad, tile_image, pad_count):
    seq_index = lax.axis_index("seq")
    seq_size, tp_size = lax.axis_size("seq"), lax.axis_size("tp")
    chunk, width = queries.shape
    lanes = width // tp_size
    row_count = chunk * tp_size
    tile_count = row_count // TILE
    packed = jnp.stack([array.reshape(chunk, tp_size, lanes) for array in (queries, keys, values, out_grad)])
    packed = packed.transpose(2, 0, 1, 3)
    doubled = jnp.concatenate([packed, packed])
    groups = [
        [seq % seq_size * tp_size + tp for seq in (left, left + 1) for tp in range(tp_size)]
        for left in range(1, seq_size, 2)
    ]
    pair = lax.all_to_all(
        doubled, ("seq", "tp"), split_axis=0, concat_axis=0, tiled=True, axis_index_groups=groups
    )
    is_right = 1 - seq_index % 2
    own = lax.dynamic_slice_in_dim(pair, is_right * tp_size, tp_size, 0)
    swaps = [(left, left + 1) for left in range(0, seq_size, 2)]
    near = lax.ppermute(own, "seq", swaps + [(right, left) for left, right in swaps])
    plan = tile_plan(tile_image, pad_count, seq_index, tile_count)
    places = jnp.stack([is_right * 2 * tp_size, (1 - is_right) * tp_size]).astype(jnp.int32)
    plan = jnp.concatenate([plan, places])
    out = jax.ShapeDtypeStruct((row_count, lanes), BF16)
    vmem = pl.BlockSpec(memory_space=pltpu.VMEM)
    return pl.pallas_call(
        attention_kernel,
        out_shape=[out] * 4,
        in_specs=[
            pl.BlockSpec(memory_space=pltpu.SMEM),
            pl.BlockSpec(memory_space=pl.ANY),
            pl.BlockSpec(memory_space=pl.ANY),
        ],
        out_specs=[vmem] * 4,
        scratch_shapes=[
            pltpu.VMEM((3 * tp_size, 4, chunk, lanes), BF16),
            pltpu.VMEM((WINDOW * TILE, WINDOW * TILE), BF16),
            pltpu.VMEM((WINDOW * TILE, WINDOW * TILE), BF16),
            pltpu.SemaphoreType.DMA((2,)),
        ],
        compiler_params=pltpu.CompilerParams(vmem_limit_bytes=32 * 1024 * 1024),
    )(plan, near, pair)


def solution(mesh):
    rows = P(("seq", "tp"), None)
    out = P("seq", "tp")
    return jax.shard_map(
        body, mesh=mesh, in_specs=(rows,) * 4 + (P(), P()), out_specs=(out,) * 4, check_vma=False
    )
```

time: 193 us -> 114 us (0.59)
  the two profiles are of different devices: /device:TPU:24 before, /device:TPU:1 now
where the time goes in v1:
time: 114 us
  waiting for transfers between devices  72 us (63%)
  starting transfers between devices  23 us (20%)
  other arithmetic  6.08 us (5%)
  Pallas kernels  6.08 us (5%)
  between operations  4.66 us (4%)
  local copies, waits for them, and re-layouts  2.3 us (2%)
    all_to_all x1, waiting for transfers between devices, body(): lax.all_to_all(doubled, ('seq', 'tp'), split_axis=0, concat_axis=0, tiled...  72 us
    all_to_all x1, starting transfers between devices, body(): lax.all_to_all(doubled, ('seq', 'tp'), split_axis=0, concat_axis=0, tiled...  16.3 us
    ppermute x1, starting transfers between devices, body(): lax.ppermute(own, 'seq', swaps + [(right, left) for left, right in swaps])  6.69 us
    pallas_call x1, Pallas kernels, body(): pl.pallas_call(attention_kernel, out_shape=[out] * 4, in_specs=[pl.BlockS...  6.08 us
  transfers between devices with their start and end apart: 2, of which 1 were waited for; matrix products, arithmetic and copies ran while one was open for 4% of the time, Pallas kernels for 0%

profile of v1, /device:TPU:1, one launch (start us, length us, event | category | flops | bytes accessed | tf_op | source)
XLA Modules:
  0.0 114.1 jit_solution(16484527455133712001)
XLA Ops:
  0.6 0.0 copy-start
  0.6 0.0 copy-start.1
  0.7 1.0 copy.18
  1.7 1.0 copy.19
  2.7 0.0 copy-done
  2.8 0.0 copy-done.1
  2.8 0.1 maximum_bitcast_fusion
  3.0 1.3 %pad_maximum_fusion = bf16[16,4,32,384]{3,2,1,0:T(8,128)(2,1)} fusion(bf16[8,4,32,384]{3,2,1,0:T(8,128)(2,1)S(1)} %maximum_bitcast_fusion), kind=kLoop, calls=%fused_computation | loop fusion | flops 786432 | bytes 2359296 | tf_op jit(solution)/shard_map/concatenate | solution.py:104
  4.3 16.3 %all-to-all-start = ((bf16[16,4,32,384]{3,2,1,0:T(8,128)(2,1)}), bf16[16,4,32,384]{3,2,1,0:T(8,128)(2,1)S(1)}, u32[]{:S(2)}, u32[]{:S(2)}) async-start(bf16[16,4,32,384]{3,2,1,0:T(8,128)(2,1)} %pad_maximum_fusion), calls=%async_computation | async-start | bytes 3145728 | tf_op jit(solution)/shard_map/all_to_all | solution.py:109
  20.6 0.0 copy-start.2
  20.6 0.0 copy-start.3
  20.6 72.0 %all-to-all-done.pair_ref = bf16[16,4,32,384]{3,2,1,0:T(8,128)(2,1)S(1)} async-done(((bf16[16,4,32,384]{3,2,1,0:T(8,128)(2,1)}), bf16[16,4,32,384]{3,2,1,0:T(8,128)(2,1)S(1)}, u32[]{:S(2)}, u32[]{:S(2)}) %all-to-all-start) | async-done | bytes 1572896 | tf_op jit(solution)/shard_map/all_to_all | solution.py:109
  92.6 0.1 constant_dynamic-slice_fusion
  92.7 6.7 %collective-permute-start = (bf16[8,4,32,384]{3,2,1,0:T(8,128)(2,1)S(1)}, bf16[8,4,32,384]{3,2,1,0:T(8,128)(2,1)S(1)}, u32[]{:S(2)}, u32[]{:S(2)}) collective-permute-start(bf16[8,4,32,384]{3,2,1,0:T(8,128)(2,1)S(1)} %constant_dynamic-slice_fusion), channel_id=1, source_target_pairs={{0,8},{16,24},{32,40},{48,56},{64,72},{80,88},{96,104},{112,120},{... | collective-permute-start | bytes 2359304 | tf_op jit(solution)/shard_map/ppermute | solution.py:115
  99.4 0.0 copy-done.2
  99.4 0.6 fusion.3
  100.1 1.9 %fusion.4 = (s32[]{:T(128)}, s32[]{:T(128)}) fusion(s32[128]{0:T(128)S(1)} %copy-done.2, s32[]{:T(128)} %get-tuple-element.8, s32[]{:T(128)} %get-tuple-element.9), kind=kLoop, calls=%fused_computation.14 | loop fusion | flops 766 | bytes 528 | tf_op jit(solution)/shard_map/reduce_sum | solution.py:29
  104.6 0.1 convert_reduce_fusion
  104.7 0.0 copy-done.3
  104.7 2.0 %fusion.5 = (s32[]{:T(128)}, s32[]{:T(128)}) fusion(s32[]{:T(128)} %get-tuple-element.8, s32[64]{0:T(128)S(1)} %copy-done.3, s32[64]{0:T(128)S(1)} %convert_reduce_fusion, s32[]{:T(128)} %get-tuple-element.9), kind=kLoop, calls=%fused_computation.15 | loop fusion | flops 510 | bytes 528 | tf_op jit(solution)/shard_map/reduce_sum | solution.py:30
  107.9 0.1 concatenate.6.plan_ref
  108.0 0.0 collective-permute-done.near_ref
  108.0 6.1 %shard_map.93 = (bf16[256,384]{1,0:T(8,128)(2,1)}, bf16[256,384]{1,0:T(8,128)(2,1)}, bf16[256,384]{1,0:T(8,128)(2,1)}, bf16[256,384]{1,0:T(8,128)(2,1)}) custom-call(s32[8]{0:T(128)S(1)} %concatenate.6.plan_ref, bf16[8,4,32,384]{3,2,1,0:T(8,128)(2,1)S(1)} %collective-permute-done.near_ref, bf16[16,4,32,384]{3,2,1,0:T(8,128)(2,1)S(1)} %all-to-all-done.pair_ref), custom_call_target="tpu_custom_call" | custom-call | tf_op jit(solution)/shard_map/pallas_call | solution.py:121
  (6 shorter events, 0.2 us)
Async XLA Ops:
  0.6 2.0 %copy-start = (bf16[32,3072]{1,0:T(8,128)(2,1)S(1)}, bf16[32,3072]{1,0:T(8,128)(2,1)}, u32[]{:S(2)}) copy-start(bf16[32,3072]{1,0:T(8,128)(2,1)} %param.8) | copy-start | bytes 589828
  0.6 2.1 %copy-start.1 = (bf16[32,3072]{1,0:T(8,128)(2,1)S(1)}, bf16[32,3072]{1,0:T(8,128)(2,1)}, u32[]{:S(2)}) copy-start(bf16[32,3072]{1,0:T(8,128)(2,1)} %param.9) | copy-start | bytes 589828
  4.3 88.3 %all-to-all-start = ((bf16[16,4,32,384]{3,2,1,0:T(8,128)(2,1)}), bf16[16,4,32,384]{3,2,1,0:T(8,128)(2,1)S(1)}, u32[]{:S(2)}, u32[]{:S(2)}) async-start(bf16[16,4,32,384]{3,2,1,0:T(8,128)(2,1)} %pad_maximum_fusion), calls=%async_computation | async-start | bytes 3145728 | tf_op jit(solution)/shard_map/all_to_all | solution.py:109
  20.6 78.8 %copy-start.2 = (s32[128]{0:T(128)S(1)}, s32[128]{0:T(128)}, u32[]{:S(2)}) copy-start(s32[128]{0:T(128)} %param.10) | copy-start | bytes 1540
  20.6 84.1 %copy-start.3 = (s32[64]{0:T(128)S(1)}, s32[64]{0:T(128)}, u32[]{:S(2)}) copy-start(s32[64]{0:T(128)} %param.11) | copy-start | bytes 772
  92.7 15.3 %collective-permute-start = (bf16[8,4,32,384]{3,2,1,0:T(8,128)(2,1)S(1)}, bf16[8,4,32,384]{3,2,1,0:T(8,128)(2,1)S(1)}, u32[]{:S(2)}, u32[]{:S(2)}) collective-permute-start(bf16[8,4,32,384]{3,2,1,0:T(8,128)(2,1)S(1)} %constant_dynamic-slice_fusion), channel_id=1, source_target_pairs={{0,8},{16,24},{32,40},{48,56},{64,72},{80,88},{96,104},{112,120},{... | collective-permute-start | bytes 2359304 | tf_op jit(solution)/shard_map/ppermute | solution.py:115

commit v2 on v1

--- a/solution.py
+++ b/solution.py
@@ -12,29 +12,30 @@
 F32 = jnp.float32
 
 
-def image_ends(tile_image, pad_count):
-    image_index = jnp.arange(pad_count.shape[0], dtype=jnp.int32)
-    stop_tiles = jnp.sum((tile_image[None, :] <= image_index[:, None]).astype(jnp.int32), axis=1)
-    return stop_tiles * TILE - pad_count
+def pack_kernel(queries_ref, keys_ref, values_ref, grads_ref, packed_ref):
+    count = packed_ref.shape[0] // 2
+    lanes = packed_ref.shape[3]
+    for index, source in enumerate((queries_ref, keys_ref, values_ref, grads_ref)):
+        for place in range(count):
+            block = source[:, place * lanes : (place + 1) * lanes]
+            packed_ref[place, index] = block
+            packed_ref[place + count, index] = block
 
 
-def tile_plan(tile_image, pad_count, seq_index, tile_count):
-    ends = image_ends(tile_image, pad_count)
-    tiles = jnp.arange(tile_image.shape[0], dtype=jnp.int32)
-    images = jnp.arange(pad_count.shape[0], dtype=jnp.int32)
-    plan = []
-    for tile in range(tile_count):
-        place = seq_index * tile_count + tile
-        image = jnp.sum(jnp.where(tiles == place, tile_image, 0))
-        first = jnp.sum((tile_image < image).astype(jnp.int32))
-        end = jnp.sum(jnp.where(images == image, ends, 0))
-        back = place - first
-        plan += [tile_count + tile - back, back, end - first * TILE]
-    return jnp.stack(plan).astype(jnp.int32)
+def image_window(tile_image_ref, pad_count_ref, place):
+    last = tile_image_ref.shape[0] - 1
+    image = tile_image_ref[place]
+
+    def same(step):
+        inside = (place + step >= 0) & (place + step <= last)
+        return (inside & (tile_image_ref[jnp.clip(place + step, 0, last)] == image)).astype(jnp.int32)
+
+    back = same(-1) + same(-2)
+    return back, (back + 1 + same(1) + same(2)) * TILE - pad_count_ref[image]
 
 
 def attention_kernel(
-    plan_ref, near_ref, pair_ref, attended_ref, query_ref, key_ref, value_ref, rows, weight_buf, grad_buf, sems
+    tile_image_ref, pad_count_ref, near_ref, pair_ref, attended_ref, query_ref, key_ref, value_ref, rows, weight_buf, grad_buf, sems
 ):
     heads = attended_ref.shape[1] // HEAD_DIM
     tile_count = attended_ref.shape[0] // TILE
@@ -42,7 +43,9 @@
     chunk = near_ref.shape[2]
     per_tile = TILE // chunk
     scaling = HEAD_DIM ** (-0.5)
-    near_at, pair_at = plan_ref[3 * tile_count], plan_ref[3 * tile_count + 1]
+    seq_index = lax.axis_index("seq")
+    is_right = 1 - lax.rem(seq_index, 2)
+    near_at, pair_at = is_right * pair_chunks, (1 - is_right) * near_chunks
     copies = (
         pltpu.make_async_copy(pair_ref, rows.at[pl.ds(pair_at, pair_chunks)], sems.at[0]),
         pltpu.make_async_copy(near_ref, rows.at[pl.ds(near_at, near_chunks)], sems.at[1]),
@@ -60,7 +63,8 @@
     column = lax.broadcasted_iota(jnp.int32, (TILE, WINDOW * TILE), 1)
     row = lax.broadcasted_iota(jnp.int32, (TILE, 1), 0)
     for tile in range(tile_count):
-        start, back, live = plan_ref[3 * tile], plan_ref[3 * tile + 1], plan_ref[3 * tile + 2]
+        back, live = image_window(tile_image_ref, pad_count_ref, seq_index * tile_count + tile)
+        start = tile_count + tile - back
         seen = column < live
         own = pl.ds(tile * TILE, TILE)
         own_window = pl.ds(pl.multiple_of(back * TILE, TILE), TILE)
@@ -98,10 +102,13 @@
     chunk, width = queries.shape
     lanes = width // tp_size
     row_count = chunk * tp_size
-    tile_count = row_count // TILE
-    packed = jnp.stack([array.reshape(chunk, tp_size, lanes) for array in (queries, keys, values, out_grad)])
-    packed = packed.transpose(2, 0, 1, 3)
-    doubled = jnp.concatenate([packed, packed])
+    vmem = pl.BlockSpec(memory_space=pltpu.VMEM)
+    doubled = pl.pallas_call(
+        pack_kernel,
+        out_shape=jax.ShapeDtypeStruct((2 * tp_size, 4, chunk, lanes), BF16),
+        in_specs=[vmem] * 4,
+        out_specs=vmem,
+    )(queries, keys, values, out_grad)
     groups = [
         [seq % seq_size * tp_size + tp for seq in (left, left + 1) for tp in range(tp_size)]
         for left in range(1, seq_size, 2)
@@ -113,15 +120,12 @@
     own = lax.dynamic_slice_in_dim(pair, is_right * tp_size, tp_size, 0)
     swaps = [(left, left + 1) for left in range(0, seq_size, 2)]
     near = lax.ppermute(own, "seq", swaps + [(right, left) for left, right in swaps])
-    plan = tile_plan(tile_image, pad_count, seq_index, tile_count)
-    places = jnp.stack([is_right * 2 * tp_size, (1 - is_right) * tp_size]).astype(jnp.int32)
-    plan = jnp.concatenate([plan, places])
     out = jax.ShapeDtypeStruct((row_count, lanes), BF16)
-    vmem = pl.BlockSpec(memory_space=pltpu.VMEM)
     return pl.pallas_call(
         attention_kernel,
         out_shape=[out] * 4,
         in_specs=[
+            pl.BlockSpec(memory_space=pltpu.SMEM),
             pl.BlockSpec(memory_space=pltpu.SMEM),
             pl.BlockSpec(memory_space=pl.ANY),
             pl.BlockSpec(memory_space=pl.ANY),
@@ -134,7 +138,7 @@
             pltpu.SemaphoreType.DMA((2,)),
         ],
         compiler_params=pltpu.CompilerParams(vmem_limit_bytes=32 * 1024 * 1024),
-    )(plan, near, pair)
+    )(tile_image, pad_count, near, pair)
 
 
 def solution(mesh):

time: 114 us -> 107 us (0.939)
  other arithmetic: 6.08 us -> 0 us
  between operations: 4.66 us -> 0.69 us
  Pallas kernels: 6.08 us -> 8.8 us
  local copies, waits for them, and re-layouts: 2.3 us -> 0.11 us
  waiting for transfers between devices: 72 us -> 73.9 us
    reduce_sum x4 -> x0, other arithmetic: 4.63 us -> none  [the longest x1 1.96 us: tile_plan(): end = jnp.sum(jnp.where(images == image, ends, 0))]
    pallas_call x0 -> x1, Pallas kernels: none -> 2.52 us  [body(): pl.pallas_call(pack_kernel, out_shape=jax.ShapeDtypeStruct((2 * tp_size,...]
    unnamed x12 -> x4, local copies, waits for them, and re-layouts: 2.03 us -> 0.01 us
    ppermute x1, waiting for transfers between devices: 0.01 us -> 1.89 us  [body(): lax.ppermute(own, 'seq', swaps + [(right, left) for left, right in swaps])]
    concatenate x1 -> x0, other arithmetic: 1.33 us -> none  [body(): doubled = jnp.concatenate([packed, packed])]
  transfers between devices with their start and end apart: 2 -> 2, of which waited for: 1 -> 2; matrix products, arithmetic and copies ran while one was open for 4% -> 0% of each run, Pallas kernels for 0% -> 0%
where the time goes in v2:
time: 107 us; the launch traced here: 106 us
  waiting for transfers between devices  73.9 us (69%)
  starting transfers between devices  23 us (21%)
  Pallas kernels  8.8 us (8%)
    all_to_all x1, waiting for transfers between devices, body(): lax.all_to_all(doubled, ('seq', 'tp'), split_axis=0, concat_axis=0, tiled...  72 us
    all_to_all x1, starting transfers between devices, body(): lax.all_to_all(doubled, ('seq', 'tp'), split_axis=0, concat_axis=0, tiled...  16.3 us
    ppermute x1, starting transfers between devices, body(): lax.ppermute(own, 'seq', swaps + [(right, left) for left, right in swaps])  6.69 us
    pallas_call x1, Pallas kernels, body(): pl.pallas_call(attention_kernel, out_shape=[out] * 4, in_specs=[pl.BlockS...  6.28 us
    pallas_call x1, Pallas kernels, body(): pl.pallas_call(pack_kernel, out_shape=jax.ShapeDtypeStruct((2 * tp_size,...  2.52 us
  transfers between devices with their start and end apart: 2, of which 2 were waited for; matrix products, arithmetic and copies ran while one was open for 0% of the time, Pallas kernels for 0%

profile of v2, /device:TPU:1, one launch (start us, length us, event | category | flops | bytes accessed | tf_op | source)
XLA Modules:
  0.0 106.5 jit_solution(17028063172240990981)
XLA Ops:
  0.6 2.5 %shard_map.93 = bf16[16,4,32,384]{3,2,1,0:T(8,128)(2,1)} custom-call(bf16[32,3072]{1,0:T(8,128)(2,1)} %queries_ref.1, bf16[32,3072]{1,0:T(8,128)(2,1)} %keys_ref.1, bf16[32,3072]{1,0:T(8,128)(2,1)} %values_ref.1, bf16[32,3072]{1,0:T(8,128)(2,1)} %grads_ref.1), custom_call_target="tpu_custom_call" | custom-call | tf_op jit(solution)/shard_map/pallas_call | solution.py:106
  3.2 16.3 %all-to-all-start = ((bf16[16,4,32,384]{3,2,1,0:T(8,128)(2,1)}), bf16[16,4,32,384]{3,2,1,0:T(8,128)(2,1)S(1)}, u32[]{:S(2)}, u32[]{:S(2)}) async-start(bf16[16,4,32,384]{3,2,1,0:T(8,128)(2,1)} %shard_map.93), calls=%async_computation | async-start | bytes 3145728 | tf_op jit(solution)/shard_map/all_to_all | solution.py:116
  19.5 0.0 copy-start
  19.5 0.0 copy-start.1
  19.5 72.0 %all-to-all-done.pair_ref = bf16[16,4,32,384]{3,2,1,0:T(8,128)(2,1)S(1)} async-done(((bf16[16,4,32,384]{3,2,1,0:T(8,128)(2,1)}), bf16[16,4,32,384]{3,2,1,0:T(8,128)(2,1)S(1)}, u32[]{:S(2)}, u32[]{:S(2)}) %all-to-all-start) | async-done | bytes 1572896 | tf_op jit(solution)/shard_map/all_to_all | solution.py:116
  91.5 0.1 constant_dynamic-slice_fusion
  91.6 6.7 %collective-permute-start = (bf16[8,4,32,384]{3,2,1,0:T(8,128)(2,1)S(1)}, bf16[8,4,32,384]{3,2,1,0:T(8,128)(2,1)S(1)}, u32[]{:S(2)}, u32[]{:S(2)}) collective-permute-start(bf16[8,4,32,384]{3,2,1,0:T(8,128)(2,1)S(1)} %constant_dynamic-slice_fusion), channel_id=1, source_target_pairs={{0,8},{16,24},{32,40},{48,56},{64,72},{80,88},{96,104},{112,120},{... | collective-permute-start | bytes 2359304 | tf_op jit(solution)/shard_map/ppermute | solution.py:122
  98.3 1.9 %collective-permute-done.near_ref = bf16[8,4,32,384]{3,2,1,0:T(8,128)(2,1)S(1)} collective-permute-done((bf16[8,4,32,384]{3,2,1,0:T(8,128)(2,1)S(1)}, bf16[8,4,32,384]{3,2,1,0:T(8,128)(2,1)S(1)}, u32[]{:S(2)}, u32[]{:S(2)}) %collective-permute-start) | collective-permute-done | bytes 786464 | tf_op jit(solution)/shard_map/ppermute | solution.py:122
  100.2 0.0 copy-done
  100.2 0.0 copy-done.1
  100.2 6.3 %shard_map.94 = (bf16[256,384]{1,0:T(8,128)(2,1)}, bf16[256,384]{1,0:T(8,128)(2,1)}, bf16[256,384]{1,0:T(8,128)(2,1)}, bf16[256,384]{1,0:T(8,128)(2,1)}) custom-call(s32[128]{0:T(128)S(1)} %copy-done, s32[64]{0:T(128)S(1)} %copy-done.1, bf16[8,4,32,384]{3,2,1,0:T(8,128)(2,1)S(1)} %collective-permute-done.near_ref, ...), custom_call_target="tpu_custom_call" | custom-call | tf_op jit(solution)/shard_map/pallas_call | solution.py:124
Async XLA Ops:
  3.2 88.3 %all-to-all-start = ((bf16[16,4,32,384]{3,2,1,0:T(8,128)(2,1)}), bf16[16,4,32,384]{3,2,1,0:T(8,128)(2,1)S(1)}, u32[]{:S(2)}, u32[]{:S(2)}) async-start(bf16[16,4,32,384]{3,2,1,0:T(8,128)(2,1)} %shard_map.93), calls=%async_computation | async-start | bytes 3145728 | tf_op jit(solution)/shard_map/all_to_all | solution.py:116
  19.5 80.7 %copy-start = (s32[128]{0:T(128)S(1)}, s32[128]{0:T(128)}, u32[]{:S(2)}) copy-start(s32[128]{0:T(128)} %tile_image_ref.1) | copy-start | bytes 1540
  19.5 80.7 %copy-start.1 = (s32[64]{0:T(128)S(1)}, s32[64]{0:T(128)}, u32[]{:S(2)}) copy-start(s32[64]{0:T(128)} %pad_count_ref.1) | copy-start | bytes 772
  91.6 8.6 %collective-permute-start = (bf16[8,4,32,384]{3,2,1,0:T(8,128)(2,1)S(1)}, bf16[8,4,32,384]{3,2,1,0:T(8,128)(2,1)S(1)}, u32[]{:S(2)}, u32[]{:S(2)}) collective-permute-start(bf16[8,4,32,384]{3,2,1,0:T(8,128)(2,1)S(1)} %constant_dynamic-slice_fusion), channel_id=1, source_target_pairs={{0,8},{16,24},{32,40},{48,56},{64,72},{80,88},{96,104},{112,120},{... | collective-permute-start | bytes 2359304 | tf_op jit(solution)/shard_map/ppermute | solution.py:122

commit v3 on v2

v3 whole, which is shorter than its diff:
```python
import jax
import jax.numpy as jnp
from jax import lax
from jax.experimental import pallas as pl
from jax.experimental.pallas import tpu as pltpu
from jax.sharding import PartitionSpec as P

HEAD_DIM = 128
TILE = 128
WINDOW = 3
LOG2_E = 1.4426950408889634
BF16 = jnp.bfloat16
F32 = jnp.float32


def pack_kernel(queries_ref, keys_ref, values_ref, grads_ref, packed_ref, rows, in_sems, out_sem):
    count = packed_ref.shape[0] // 2
    lanes = packed_ref.shape[3]
    sources = (queries_ref, keys_ref, values_ref, grads_ref)
    loads = [pltpu.make_async_copy(source, rows.at[index], in_sems.at[index]) for index, source in enumerate(sources)]
    for load in loads:
        load.start()
    for index, load in enumerate(loads):
        load.wait()
        for place in range(2 * count):
            block = rows.at[index, :, pl.ds(place % count * lanes, lanes)]
            pltpu.make_async_copy(block, packed_ref.at[place, index], out_sem).start()
    pltpu.make_async_copy(packed_ref, packed_ref, out_sem).wait()


def image_window(tile_image_ref, pad_count_ref, place):
    last = tile_image_ref.shape[0] - 1
    image = tile_image_ref[place]

    def same(step):
        inside = (place + step >= 0) & (place + step <= last)
        return (inside & (tile_image_ref[jnp.clip(place + step, 0, last)] == image)).astype(jnp.int32)

    back = same(-1) + same(-2)
    return back, (back + 1 + same(1) + same(2)) * TILE - pad_count_ref[image]


def attention_kernel(
    tile_image_ref,
    pad_count_ref,
    near_ref,
    pair_ref,
    attended_ref,
    query_ref,
    key_ref,
    value_ref,
    rows,
    weight_buf,
    grad_buf,
    sems,
):
    heads = attended_ref.shape[1] // HEAD_DIM
    tile_count = attended_ref.shape[0] // TILE
    near_chunks, pair_chunks = near_ref.shape[0], pair_ref.shape[0]
    chunk = near_ref.shape[2]
    per_tile = TILE // chunk
    scaling = HEAD_DIM ** (-0.5)
    seq_index = lax.axis_index("seq")
    is_right = 1 - lax.rem(seq_index, 2)
    near_at, pair_at = is_right * pair_chunks, (1 - is_right) * near_chunks
    copies = (
        pltpu.make_async_copy(pair_ref, rows.at[pl.ds(pair_at, pair_chunks)], sems.at[0]),
        pltpu.make_async_copy(near_ref, rows.at[pl.ds(near_at, near_chunks)], sems.at[1]),
    )
    for copy in copies:
        copy.start()
    windows = []
    for tile in range(tile_count):
        back, live = image_window(tile_image_ref, pad_count_ref, seq_index * tile_count + tile)
        windows.append((tile_count + tile - back, back, live))
    for copy in copies:
        copy.wait()
    contract_last = (((1,), (1,)), ((), ()))
    contract_first = (((0,), (0,)), ((), ()))

    def dot(left, right, dims):
        return lax.dot_general(left, right, dims, preferred_element_type=F32)

    key_row = lax.broadcasted_iota(jnp.int32, (WINDOW * TILE, TILE), 0)
    query_lane = lax.broadcasted_iota(jnp.int32, (1, TILE), 1)

    def place(item):
        head, tile = divmod(item, tile_count)
        start, back, live = windows[tile]
        lanes = slice(head * HEAD_DIM, (head + 1) * HEAD_DIM)
        slab = pl.ds(start * per_tile, WINDOW * per_tile)
        parts = [rows[slab, index, :, lanes].reshape(WINDOW * TILE, HEAD_DIM) for index in range(4)]
        return tile, back, live, lanes, parts, item % 2

    def weigh(item):
        _, _, live, _, (queries, keys, values, grads), slot = place(item)
        for step in range(WINDOW):
            across = slice(step * TILE, (step + 1) * TILE)
            scores = jnp.where(key_row < live, dot(keys, queries[across], contract_last), -1e30)
            value_score = dot(values, grads[across], contract_last)
            top = jnp.max(scores, axis=0, keepdims=True)
            raised = jnp.exp2((scores - top) * (scaling * LOG2_E))
            total = jnp.sum(raised, axis=0, keepdims=True)
            weights = raised * jnp.where(query_lane + step * TILE < live, 1.0 / total, 0.0)
            grad_dot = jnp.sum(weights * value_score, axis=0, keepdims=True)
            weight_buf[slot, :, across] = weights.astype(BF16)
            grad_buf[slot, :, across] = (weights * (value_score - grad_dot)).astype(BF16)

    def collect(item):
        tile, back, _, lanes, (queries, keys, values, grads), slot = place(item)
        own = slice(tile * TILE, (tile + 1) * TILE)
        inside = pl.ds(pl.multiple_of(back * TILE, TILE), TILE)
        attended_ref[own, lanes] = dot(weight_buf[slot, :, inside], values, contract_first).astype(BF16)
        query_ref[own, lanes] = (dot(grad_buf[slot, :, inside], keys, contract_first) * scaling).astype(BF16)
        key_sum = jnp.dot(grad_buf[slot, inside, :], queries, preferred_element_type=F32)
        key_ref[own, lanes] = (key_sum * scaling).astype(BF16)
        value_sum = jnp.dot(weight_buf[slot, inside, :], grads, preferred_element_type=F32)
        value_ref[own, lanes] = value_sum.astype(BF16)

    items = heads * tile_count
    for item in range(items + 1):
        if item < items:
            weigh(item)
        if item > 0:
            collect(item - 1)


def body(queries, keys, values, out_grad, tile_image, pad_count):
    seq_index = lax.axis_index("seq")
    seq_size, tp_size = lax.axis_size("seq"), lax.axis_size("tp")
    chunk, width = queries.shape
    lanes = width // tp_size
    row_count = chunk * tp_size
    vmem = pl.BlockSpec(memory_space=pltpu.VMEM)
    anywhere = pl.BlockSpec(memory_space=pl.ANY)
    doubled = pl.pallas_call(
        pack_kernel,
        out_shape=jax.ShapeDtypeStruct((2 * tp_size, 4, chunk, lanes), BF16),
        in_specs=[anywhere] * 4,
        out_specs=anywhere,
        scratch_shapes=[
            pltpu.VMEM((4, chunk, width), BF16),
            pltpu.SemaphoreType.DMA((4,)),
            pltpu.SemaphoreType.DMA,
        ],
    )(queries, keys, values, out_grad)
    groups = [
        [seq % seq_size * tp_size + tp for seq in (left, left + 1) for tp in range(tp_size)]
        for left in range(1, seq_size, 2)
    ]
    pair = lax.all_to_all(
        doubled, ("seq", "tp"), split_axis=0, concat_axis=0, tiled=True, axis_index_groups=groups
    )
    is_right = 1 - seq_index % 2
    own = lax.dynamic_slice_in_dim(pair, is_right * tp_size, tp_size, 0)
    swaps = [(left, left + 1) for left in range(0, seq_size, 2)]
    near = lax.ppermute(own, "seq", swaps + [(right, left) for left, right in swaps])
    out = jax.ShapeDtypeStruct((row_count, lanes), BF16)
    return pl.pallas_call(
        attention_kernel,
        out_shape=[out] * 4,
        in_specs=[
            pl.BlockSpec(memory_space=pltpu.SMEM),
            pl.BlockSpec(memory_space=pltpu.SMEM),
            anywhere,
            anywhere,
        ],
        out_specs=[vmem] * 4,
        scratch_shapes=[
            pltpu.VMEM((3 * tp_size, 4, chunk, lanes), BF16),
            pltpu.VMEM((2, WINDOW * TILE, WINDOW * TILE), BF16),
            pltpu.VMEM((2, WINDOW * TILE, WINDOW * TILE), BF16),
            pltpu.SemaphoreType.DMA((2,)),
        ],
        compiler_params=pltpu.CompilerParams(vmem_limit_bytes=32 * 1024 * 1024),
    )(tile_image, pad_count, near, pair)


def solution(mesh):
    rows = P(("seq", "tp"), None)
    out = P("seq", "tp")
    return jax.shard_map(
        body, mesh=mesh, in_specs=(rows,) * 4 + (P(), P()), out_specs=(out,) * 4, check_vma=False
    )
```

time: 107 us -> 105 us (0.981)
  Pallas kernels: 8.8 us -> 7.27 us
    pallas_call x1, Pallas kernels: 6.28 us -> 5.11 us  [body(): pl.pallas_call(attention_kernel, out_shape=[out] * 4, in_specs=[pl.BlockS...]
where the time goes in v3:
time: 105 us
  waiting for transfers between devices  73.9 us (70%)
  starting transfers between devices  23 us (22%)
  Pallas kernels  7.27 us (7%)
    all_to_all x1, waiting for transfers between devices, body(): lax.all_to_all(doubled, ('seq', 'tp'), split_axis=0, concat_axis=0, tiled...  72 us
    all_to_all x1, starting transfers between devices, body(): lax.all_to_all(doubled, ('seq', 'tp'), split_axis=0, concat_axis=0, tiled...  16.3 us
    ppermute x1, starting transfers between devices, body(): lax.ppermute(own, 'seq', swaps + [(right, left) for left, right in swaps])  6.69 us
    pallas_call x1, Pallas kernels, body(): pl.pallas_call(attention_kernel, out_shape=[out] * 4, in_specs=[pl.BlockS...  5.11 us
    pallas_call x1, Pallas kernels, body(): pl.pallas_call(pack_kernel, out_shape=jax.ShapeDtypeStruct((2 * tp_size,...  2.15 us
  transfers between devices with their start and end apart: 2, of which 2 were waited for; matrix products, arithmetic and copies ran while one was open for 0% of the time, Pallas kernels for 0%

profile of v3, /device:TPU:1, one launch (start us, length us, event | category | flops | bytes accessed | tf_op | source)
XLA Modules:
  0.0 105.0 jit_solution(15336351577840473283)
XLA Ops:
  0.6 2.2 %shard_map.93 = bf16[16,4,32,384]{3,2,1,0:T(8,128)(2,1)} custom-call(bf16[32,3072]{1,0:T(8,128)(2,1)} %queries_ref.1, bf16[32,3072]{1,0:T(8,128)(2,1)} %keys_ref.1, bf16[32,3072]{1,0:T(8,128)(2,1)} %values_ref.1, bf16[32,3072]{1,0:T(8,128)(2,1)} %grads_ref.1), custom_call_target="tpu_custom_call" | custom-call | tf_op jit(solution)/shard_map/pallas_call | solution.py:136
  2.8 16.3 %all-to-all-start = ((bf16[16,4,32,384]{3,2,1,0:T(8,128)(2,1)}), bf16[16,4,32,384]{3,2,1,0:T(8,128)(2,1)S(1)}, u32[]{:S(2)}, u32[]{:S(2)}) async-start(bf16[16,4,32,384]{3,2,1,0:T(8,128)(2,1)} %shard_map.93), calls=%async_computation | async-start | bytes 3145728 | tf_op jit(solution)/shard_map/all_to_all | solution.py:151
  19.1 0.0 copy-start
  19.1 0.0 copy-start.1
  19.2 72.0 %all-to-all-done.pair_ref = bf16[16,4,32,384]{3,2,1,0:T(8,128)(2,1)S(1)} async-done(((bf16[16,4,32,384]{3,2,1,0:T(8,128)(2,1)}), bf16[16,4,32,384]{3,2,1,0:T(8,128)(2,1)S(1)}, u32[]{:S(2)}, u32[]{:S(2)}) %all-to-all-start) | async-done | bytes 1572896 | tf_op jit(solution)/shard_map/all_to_all | solution.py:151
  91.2 0.1 constant_dynamic-slice_fusion
  91.3 6.7 %collective-permute-start = (bf16[8,4,32,384]{3,2,1,0:T(8,128)(2,1)S(1)}, bf16[8,4,32,384]{3,2,1,0:T(8,128)(2,1)S(1)}, u32[]{:S(2)}, u32[]{:S(2)}) collective-permute-start(bf16[8,4,32,384]{3,2,1,0:T(8,128)(2,1)S(1)} %constant_dynamic-slice_fusion), channel_id=1, source_target_pairs={{0,8},{16,24},{32,40},{48,56},{64,72},{80,88},{96,104},{112,120},{... | collective-permute-start | bytes 2359304 | tf_op jit(solution)/shard_map/ppermute | solution.py:157
  97.9 1.9 %collective-permute-done.near_ref = bf16[8,4,32,384]{3,2,1,0:T(8,128)(2,1)S(1)} collective-permute-done((bf16[8,4,32,384]{3,2,1,0:T(8,128)(2,1)S(1)}, bf16[8,4,32,384]{3,2,1,0:T(8,128)(2,1)S(1)}, u32[]{:S(2)}, u32[]{:S(2)}) %collective-permute-start) | collective-permute-done | bytes 786464 | tf_op jit(solution)/shard_map/ppermute | solution.py:157
  99.8 0.0 copy-done
  99.8 0.0 copy-done.1
  99.8 5.1 %shard_map.94 = (bf16[256,384]{1,0:T(8,128)(2,1)}, bf16[256,384]{1,0:T(8,128)(2,1)}, bf16[256,384]{1,0:T(8,128)(2,1)}, bf16[256,384]{1,0:T(8,128)(2,1)}) custom-call(s32[128]{0:T(128)S(1)} %copy-done, s32[64]{0:T(128)S(1)} %copy-done.1, bf16[8,4,32,384]{3,2,1,0:T(8,128)(2,1)S(1)} %collective-permute-done.near_ref, ...), custom_call_target="tpu_custom_call" | custom-call | tf_op jit(solution)/shard_map/pallas_call | solution.py:159
Async XLA Ops:
  2.8 88.4 %all-to-all-start = ((bf16[16,4,32,384]{3,2,1,0:T(8,128)(2,1)}), bf16[16,4,32,384]{3,2,1,0:T(8,128)(2,1)S(1)}, u32[]{:S(2)}, u32[]{:S(2)}) async-start(bf16[16,4,32,384]{3,2,1,0:T(8,128)(2,1)} %shard_map.93), calls=%async_computation | async-start | bytes 3145728 | tf_op jit(solution)/shard_map/all_to_all | solution.py:151
  19.1 80.7 %copy-start = (s32[128]{0:T(128)S(1)}, s32[128]{0:T(128)}, u32[]{:S(2)}) copy-start(s32[128]{0:T(128)} %tile_image_ref.1) | copy-start | bytes 1540
  19.1 80.7 %copy-start.1 = (s32[64]{0:T(128)S(1)}, s32[64]{0:T(128)}, u32[]{:S(2)}) copy-start(s32[64]{0:T(128)} %pad_count_ref.1) | copy-start | bytes 772
  91.3 8.6 %collective-permute-start = (bf16[8,4,32,384]{3,2,1,0:T(8,128)(2,1)S(1)}, bf16[8,4,32,384]{3,2,1,0:T(8,128)(2,1)S(1)}, u32[]{:S(2)}, u32[]{:S(2)}) collective-permute-start(bf16[8,4,32,384]{3,2,1,0:T(8,128)(2,1)S(1)} %constant_dynamic-slice_fusion), channel_id=1, source_target_pairs={{0,8},{16,24},{32,40},{48,56},{64,72},{80,88},{96,104},{112,120},{... | collective-permute-start | bytes 2359304 | tf_op jit(solution)/shard_map/ppermute | solution.py:157

commit v4 on v3

--- a/solution.py
+++ b/solution.py
@@ -13,13 +13,21 @@
 F32 = jnp.float32
 
 
-def pack_kernel(queries_ref, keys_ref, values_ref, grads_ref, packed_ref, rows, in_sems, out_sem):
+def pack_kernel(
+    tile_image_ref, queries_ref, keys_ref, values_ref, grads_ref, packed_ref, shared_ref, rows, in_sems, out_sem
+):
     count = packed_ref.shape[0] // 2
     lanes = packed_ref.shape[3]
     sources = (queries_ref, keys_ref, values_ref, grads_ref)
     loads = [pltpu.make_async_copy(source, rows.at[index], in_sems.at[index]) for index, source in enumerate(sources)]
     for load in loads:
         load.start()
+    last = tile_image_ref.shape[0] - 1
+    tile_count = count * queries_ref.shape[0] // TILE
+    seq_index = lax.axis_index("seq")
+    after = (seq_index + lax.rem(seq_index, 2)) * tile_count
+    joined = tile_image_ref[jnp.clip(after - 1, 0, last)] == tile_image_ref[jnp.clip(after, 0, last)]
+    shared_ref[0] = ((after > 0) & (after <= last) & joined).astype(jnp.int32)
     for index, load in enumerate(loads):
         load.wait()
         for place in range(2 * count):
@@ -132,25 +140,37 @@
     lanes = width // tp_size
     row_count = chunk * tp_size
     vmem = pl.BlockSpec(memory_space=pltpu.VMEM)
+    smem = pl.BlockSpec(memory_space=pltpu.SMEM)
     anywhere = pl.BlockSpec(memory_space=pl.ANY)
-    doubled = pl.pallas_call(
+    doubled, shared = pl.pallas_call(
         pack_kernel,
-        out_shape=jax.ShapeDtypeStruct((2 * tp_size, 4, chunk, lanes), BF16),
-        in_specs=[anywhere] * 4,
-        out_specs=anywhere,
+        out_shape=[
+            jax.ShapeDtypeStruct((2 * tp_size, 4, chunk, lanes), BF16),
+            jax.ShapeDtypeStruct((1,), jnp.int32),
+        ],
+        in_specs=[smem] + [anywhere] * 4,
+        out_specs=[anywhere, smem],
         scratch_shapes=[
             pltpu.VMEM((4, chunk, width), BF16),
             pltpu.SemaphoreType.DMA((4,)),
             pltpu.SemaphoreType.DMA,
         ],
-    )(queries, keys, values, out_grad)
+    )(tile_image, queries, keys, values, out_grad)
     groups = [
         [seq % seq_size * tp_size + tp for seq in (left, left + 1) for tp in range(tp_size)]
         for left in range(1, seq_size, 2)
     ]
-    pair = lax.all_to_all(
-        doubled, ("seq", "tp"), split_axis=0, concat_axis=0, tiled=True, axis_index_groups=groups
-    )
+
+    def with_far(chunks):
+        return lax.all_to_all(
+            chunks, ("seq", "tp"), split_axis=0, concat_axis=0, tiled=True, axis_index_groups=groups
+        )
+
+    def own_only(chunks):
+        mine = lax.all_to_all(chunks[:tp_size], "tp", split_axis=0, concat_axis=0, tiled=True)
+        return jnp.concatenate([mine, mine])
+
+    pair = lax.cond(shared[0] > 0, with_far, own_only, doubled)
     is_right = 1 - seq_index % 2
     own = lax.dynamic_slice_in_dim(pair, is_right * tp_size, tp_size, 0)
     swaps = [(left, left + 1) for left in range(0, seq_size, 2)]
@@ -160,8 +180,8 @@
         attention_kernel,
         out_shape=[out] * 4,
         in_specs=[
-            pl.BlockSpec(memory_space=pltpu.SMEM),
-            pl.BlockSpec(memory_space=pltpu.SMEM),
+            smem,
+            smem,
             anywhere,
             anywhere,
         ],

time: 105 us -> 103 us (0.981)
  the two profiles are of different devices: /device:TPU:1 before, /device:TPU:39 now
where the time goes in v4:
time: 103 us
  blocking collectives  81.8 us (79%)
  starting transfers between devices  10 us (10%)
  Pallas kernels  7.49 us (7%)
  waiting for transfers between devices  1.89 us (2%)
  between operations  1.33 us (1%)
    all_to_all x1, blocking collectives, with_far(): lax.all_to_all(chunks, ('seq', 'tp'), split_axis=0, concat_axis=0, tiled=...  81.8 us
    ppermute x1, starting transfers between devices, body(): lax.ppermute(own, 'seq', swaps + [(right, left) for left, right in swaps])  10 us
    pallas_call x1, Pallas kernels, body(): pl.pallas_call(attention_kernel, out_shape=[out] * 4, in_specs=[smem, sme...  4.93 us
    pallas_call x1, Pallas kernels, body(): pl.pallas_call(pack_kernel, out_shape=[jax.ShapeDtypeStruct((2 * tp_size,...  2.55 us
  transfers between devices with their start and end apart: 1, of which 1 were waited for; matrix products, arithmetic and copies ran while one was open for 0% of the time, Pallas kernels for 0%

profile of v4, /device:TPU:39, one launch (start us, length us, event | category | flops | bytes accessed | tf_op | source)
XLA Modules:
  0.0 102.6 jit_solution(12119725305636452573)
XLA Ops:
  0.6 2.6 %shard_map.93 = (bf16[16,4,32,384]{3,2,1,0:T(8,128)(2,1)S(1)}, s32[1]{0:T(128)}) custom-call(s32[128]{0:T(128)} %tile_image_ref.3, bf16[32,3072]{1,0:T(8,128)(2,1)} %queries_ref.1, bf16[32,3072]{1,0:T(8,128)(2,1)} %keys_ref.1, bf16[32,3072]{1,0:T(8,128)(2,1)} %values_ref.1, bf16[32,3072]{1,0:T(8,128)(2,1)} %grads_ref.1), custom_call_target="tpu_custom_call" | custom-call | tf_op jit(solution)/shard_map/pallas_call | solution.py:145
  3.9 81.8 %conditional.1 = (bf16[16,4,32,384]{3,2,1,0:T(8,128)(2,1)S(1)}) conditional(s32[]{:T(128)} %bitcast, bf16[16,4,32,384]{3,2,1,0:T(8,128)(2,1)S(1)} %get-tuple-element.12, bf16[16,4,32,384]{3,2,1,0:T(8,128)(2,1)S(1)} %get-tuple-element.12), branch_computations={%region_0.0_spmd, %region_1.0_spmd} | conditional | flops 786432 | bytes 5505032 | solution.py:173
  3.9 81.8 %all_to_all.9 = bf16[16,4,32,384]{3,2,1,0:T(8,128)(2,1)S(1)} all-to-all(bf16[16,4,32,384]{3,2,1,0:T(8,128)(2,1)S(1)} %param.1), channel_id=1, replica_groups={{8,9,10,11,12,13,14,15,16,17,18,19,20,21,22,23},{24,25,26,27,28,29,30,3..., dimensions={0} | all-to-all | bytes 3145728 | tf_op jit(solution)/shard_map/cond/branch_1_fun/all_to_all | solution.py:165
  85.7 0.0 copy-start
  85.7 0.0 copy-start.1
  85.7 0.1 constant_dynamic-slice_fusion
  85.8 10.0 %collective-permute-start = (bf16[8,4,32,384]{3,2,1,0:T(8,128)(2,1)S(1)}, bf16[8,4,32,384]{3,2,1,0:T(8,128)(2,1)S(1)}, u32[]{:S(2)}, u32[]{:S(2)}) collective-permute-start(bf16[8,4,32,384]{3,2,1,0:T(8,128)(2,1)S(1)} %constant_dynamic-slice_fusion), channel_id=1, source_target_pairs={{0,8},{16,24},{32,40},{48,56},{64,72},{80,88},{96,104},{112,120},{... | collective-permute-start | bytes 2359304 | tf_op jit(solution)/shard_map/ppermute | solution.py:177
  95.8 1.9 %collective-permute-done.near_ref = bf16[8,4,32,384]{3,2,1,0:T(8,128)(2,1)S(1)} collective-permute-done((bf16[8,4,32,384]{3,2,1,0:T(8,128)(2,1)S(1)}, bf16[8,4,32,384]{3,2,1,0:T(8,128)(2,1)S(1)}, u32[]{:S(2)}, u32[]{:S(2)}) %collective-permute-start) | collective-permute-done | bytes 786464 | tf_op jit(solution)/shard_map/ppermute | solution.py:177
  97.7 0.0 copy-done
  97.7 0.0 copy-done.1
  97.7 4.9 %shard_map.94 = (bf16[256,384]{1,0:T(8,128)(2,1)}, bf16[256,384]{1,0:T(8,128)(2,1)}, bf16[256,384]{1,0:T(8,128)(2,1)}, bf16[256,384]{1,0:T(8,128)(2,1)}) custom-call(s32[128]{0:T(128)S(1)} %copy-done, s32[64]{0:T(128)S(1)} %copy-done.1, bf16[8,4,32,384]{3,2,1,0:T(8,128)(2,1)S(1)} %collective-permute-done.near_ref, ...), custom_call_target="tpu_custom_call" | custom-call | tf_op jit(solution)/shard_map/pallas_call | solution.py:179
Async XLA Ops:
  85.7 12.0 %copy-start = (s32[128]{0:T(128)S(1)}, s32[128]{0:T(128)}, u32[]{:S(2)}) copy-start(s32[128]{0:T(128)} %tile_image_ref.3) | copy-start | bytes 1540
  85.7 12.0 %copy-start.1 = (s32[64]{0:T(128)S(1)}, s32[64]{0:T(128)}, u32[]{:S(2)}) copy-start(s32[64]{0:T(128)} %pad_count_ref.1) | copy-start | bytes 772
  85.8 11.9 %collective-permute-start = (bf16[8,4,32,384]{3,2,1,0:T(8,128)(2,1)S(1)}, bf16[8,4,32,384]{3,2,1,0:T(8,128)(2,1)S(1)}, u32[]{:S(2)}, u32[]{:S(2)}) collective-permute-start(bf16[8,4,32,384]{3,2,1,0:T(8,128)(2,1)S(1)} %constant_dynamic-slice_fusion), channel_id=1, source_target_pairs={{0,8},{16,24},{32,40},{48,56},{64,72},{80,88},{96,104},{112,120},{... | collective-permute-start | bytes 2359304 | tf_op jit(solution)/shard_map/ppermute | solution.py:177

commit v5 on v4

v5 whole, which is shorter than its diff:
```python
import jax
import jax.numpy as jnp
from jax import lax
from jax.experimental import pallas as pl
from jax.experimental.pallas import tpu as pltpu
from jax.sharding import PartitionSpec as P

HEAD_DIM = 128
TILE = 128
WINDOW = 3
LOG2_E = 1.4426950408889634
BF16 = jnp.bfloat16
F32 = jnp.float32


def pack_kernel(
    tile_image_ref,
    queries_ref,
    keys_ref,
    values_ref,
    grads_ref,
    packed_ref,
    shared_ref,
    rows,
    images,
    shared,
    in_sems,
    out_sem,
    scalar_sems,
):
    count = packed_ref.shape[0] // 2
    lanes = packed_ref.shape[3]
    sources = (queries_ref, keys_ref, values_ref, grads_ref)
    fetch = pltpu.make_async_copy(tile_image_ref, images, scalar_sems.at[0])
    fetch.start()
    loads = [pltpu.make_async_copy(source, rows.at[index], in_sems.at[index]) for index, source in enumerate(sources)]
    for load in loads:
        load.start()
    last = tile_image_ref.shape[0] - 1
    tile_count = count * queries_ref.shape[0] // TILE
    seq_index = lax.axis_index("seq")
    after = (seq_index + lax.rem(seq_index, 2)) * tile_count
    fetch.wait()
    joined = images[jnp.clip(after - 1, 0, last)] == images[jnp.clip(after, 0, last)]
    shared[0] = ((after > 0) & (after <= last) & joined).astype(jnp.int32)
    tell = pltpu.make_async_copy(shared, shared_ref, scalar_sems.at[1])
    tell.start()
    for index, load in enumerate(loads):
        load.wait()
        for place in range(2 * count):
            block = rows.at[index, :, pl.ds(place % count * lanes, lanes)]
            pltpu.make_async_copy(block, packed_ref.at[place, index], out_sem).start()
    pltpu.make_async_copy(packed_ref, packed_ref, out_sem).wait()
    tell.wait()


def image_window(tile_image_ref, pad_count_ref, place):
    last = tile_image_ref.shape[0] - 1
    image = tile_image_ref[place]

    def same(step):
        inside = (place + step >= 0) & (place + step <= last)
        return (inside & (tile_image_ref[jnp.clip(place + step, 0, last)] == image)).astype(jnp.int32)

    back = same(-1) + same(-2)
    return back, (back + 1 + same(1) + same(2)) * TILE - pad_count_ref[image]


def dot(left, right, dims):
    return lax.dot_general(left, right, dims, preferred_element_type=F32)


def attend(heads, load, first_live, live, weight_buf, grad_buf, stores):
    scaling = HEAD_DIM ** (-0.5)
    contract_last = (((1,), (1,)), ((), ()))
    contract_first = (((0,), (0,)), ((), ()))
    key_row = lax.broadcasted_iota(jnp.int32, (WINDOW * TILE, TILE), 0)
    query_lane = lax.broadcasted_iota(jnp.int32, (1, TILE), 1)

    def inside(places):
        return (places >= first_live) & (places < first_live + live)

    def weigh(head):
        queries, keys, values, grads = load(head)
        for step in range(WINDOW):
            across = slice(step * TILE, (step + 1) * TILE)
            scores = jnp.where(inside(key_row), dot(keys, queries[across], contract_last), -1e30)
            value_score = dot(values, grads[across], contract_last)
            top = jnp.max(scores, axis=0, keepdims=True)
            raised = jnp.exp2((scores - top) * (scaling * LOG2_E))
            total = jnp.sum(raised, axis=0, keepdims=True)
            weights = raised * jnp.where(inside(query_lane + step * TILE), 1.0 / total, 0.0)
            grad_dot = jnp.sum(weights * value_score, axis=0, keepdims=True)
            weight_buf[head, :, across] = weights.astype(BF16)
            grad_buf[head, :, across] = (weights * (value_score - grad_dot)).astype(BF16)

    def collect(head, at, store):
        queries, keys, values, grads = load(head)
        own = pl.ds(pl.multiple_of(at * TILE, TILE), TILE)
        attended = dot(weight_buf[head, :, own], values, contract_first)
        query_sum = dot(grad_buf[head, :, own], keys, contract_first)
        key_sum = jnp.dot(grad_buf[head, own, :], queries, preferred_element_type=F32)
        value_sum = jnp.dot(weight_buf[head, own, :], grads, preferred_element_type=F32)
        results = (attended, query_sum * scaling, key_sum * scaling, value_sum)
        store(head, [result.astype(BF16) for result in results])

    (at, store), *others = stores
    for head in range(heads + 1):
        if head < heads:
            weigh(head)
        if head > 0:
            collect(head - 1, at, store)
    for wanted, at, store in others:

        @pl.when(wanted)
        def _():
            for head in range(heads):
                collect(head, at, store)


def head_lanes(head):
    return slice(head * HEAD_DIM, (head + 1) * HEAD_DIM)


def near_tile(is_right):
    return is_right, 3 * is_right - 1


def spans_near(tile_image_ref, first_tile, is_right):
    last = tile_image_ref.shape[0] - 1
    mine, beyond = near_tile(is_right)
    beyond = first_tile + beyond
    same = tile_image_ref[first_tile + mine] == tile_image_ref[jnp.clip(beyond, 0, last)]
    return (beyond >= 0) & (beyond <= last) & same


def far_kernel(
    tile_image_ref, pad_count_ref, pair_ref, attended_ref, query_ref, key_ref, value_ref, weight_buf, grad_buf
):
    heads = attended_ref.shape[1] // HEAD_DIM
    tile_count = attended_ref.shape[0] // TILE
    per_tile = TILE // pair_ref.shape[2]
    seq_index = lax.axis_index("seq")
    is_right = 1 - lax.rem(seq_index, 2)
    first_tile = seq_index * tile_count
    near_image = tile_image_ref[first_tile + near_tile(is_right)[0]]
    spans = spans_near(tile_image_ref, first_tile, is_right)
    outs = (attended_ref, query_ref, key_ref, value_ref)
    for tile in range(tile_count):
        back, live = image_window(tile_image_ref, pad_count_ref, first_tile + tile)
        place = tile_count * is_right + tile
        start = jnp.minimum(place - back, 1)

        def load(head):
            slab = pl.ds(start * per_tile, WINDOW * per_tile)
            lanes = head_lanes(head)
            return [pair_ref[slab, index, :, lanes].reshape(WINDOW * TILE, HEAD_DIM) for index in range(4)]

        def store(head, results):
            for out, result in zip(outs, results):
                out[tile * TILE : (tile + 1) * TILE, head_lanes(head)] = result

        @pl.when(jnp.logical_not(spans & (tile_image_ref[first_tile + tile] == near_image)))
        def _():
            first_live = (place - back - start) * TILE
            attend(heads, load, first_live, live, weight_buf, grad_buf, [(place - start, store)])


def near_kernel(
    tile_image_ref,
    pad_count_ref,
    near_ref,
    pair_ref,
    attended_in,
    query_in,
    key_in,
    value_in,
    attended_ref,
    query_ref,
    key_ref,
    value_ref,
    results,
    weight_buf,
    grad_buf,
    sems,
):
    del attended_in, query_in, key_in, value_in
    heads = attended_ref.shape[1] // HEAD_DIM
    tile_count = attended_ref.shape[0] // TILE
    per_tile = TILE // pair_ref.shape[2]
    seq_index = lax.axis_index("seq")
    is_right = 1 - lax.rem(seq_index, 2)
    first_tile = seq_index * tile_count
    outs = (attended_ref, query_ref, key_ref, value_ref)
    main = near_tile(is_right)[0]
    other = 1 - main
    back, live = image_window(tile_image_ref, pad_count_ref, first_tile + main)
    place = main + tile_count * (1 - is_right)
    start = place - back
    both = tile_image_ref[first_tile] == tile_image_ref[first_tile + 1]

    def load(head):
        parts = []
        for index in range(4):
            tiles = []
            for step in range(WINDOW):
                lower = start + step < tile_count
                from_near = lower == (is_right == 0)
                within = lax.rem(start + step, tile_count)
                near_slab = pl.ds(within * per_tile, per_tile)
                own_slab = pl.ds((within + tile_count * is_right) * per_tile, per_tile)
                lanes = head_lanes(head)
                tile = jnp.where(from_near, near_ref[near_slab, index, :, lanes], pair_ref[own_slab, index, :, lanes])
                tiles.append(tile.reshape(TILE, HEAD_DIM))
            parts.append(jnp.concatenate(tiles))
        return parts

    def store_at(slot):
        def store(head, values):
            for index, value in enumerate(values):
                results[slot, index, :, head_lanes(head)] = value

        return store

    def copies(slot, tile):
        rows = pl.ds(pl.multiple_of(tile * TILE, TILE), TILE)
        return [
            pltpu.make_async_copy(results.at[slot, index], out.at[rows], sems.at[slot, index])
            for index, out in enumerate(outs)
        ]

    @pl.when(spans_near(tile_image_ref, first_tile, is_right))
    def _():
        stores = [(place - start, store_at(0)), (both, place - start + other - main, store_at(1))]
        attend(heads, load, 0, live, weight_buf, grad_buf, stores)
        for copy in copies(0, main):
            copy.start()

        @pl.when(both)
        def _():
            for copy in copies(1, other):
                copy.start()
            for copy in copies(1, other):
                copy.wait()

        for copy in copies(0, main):
            copy.wait()


def body(queries, keys, values, out_grad, tile_image, pad_count):
    seq_index = lax.axis_index("seq")
    seq_size, tp_size = lax.axis_size("seq"), lax.axis_size("tp")
    chunk, width = queries.shape
    lanes = width // tp_size
    row_count = chunk * tp_size
    vmem = pl.BlockSpec(memory_space=pltpu.VMEM)
    smem = pl.BlockSpec(memory_space=pltpu.SMEM)
    anywhere = pl.BlockSpec(memory_space=pl.ANY)
    doubled, shared = pl.pallas_call(
        pack_kernel,
        out_shape=[
            jax.ShapeDtypeStruct((2 * tp_size, 4, chunk, lanes), BF16),
            jax.ShapeDtypeStruct((1,), jnp.int32),
        ],
        in_specs=[anywhere] * 5,
        out_specs=[anywhere] * 2,
        scratch_shapes=[
            pltpu.VMEM((4, chunk, width), BF16),
            pltpu.SMEM(tile_image.shape, jnp.int32),
            pltpu.SMEM((1,), jnp.int32),
            pltpu.SemaphoreType.DMA((4,)),
            pltpu.SemaphoreType.DMA,
            pltpu.SemaphoreType.DMA((2,)),
        ],
    )(tile_image, queries, keys, values, out_grad)
    groups = [
        [seq % seq_size * tp_size + tp for seq in (left, left + 1) for tp in range(tp_size)]
        for left in range(1, seq_size, 2)
    ]

    def with_far(chunks):
        return lax.all_to_all(
            chunks, ("seq", "tp"), split_axis=0, concat_axis=0, tiled=True, axis_index_groups=groups
        )

    def own_only(chunks):
        mine = lax.all_to_all(chunks[:tp_size], "tp", split_axis=0, concat_axis=0, tiled=True)
        return jnp.concatenate([mine, mine])

    pair = lax.cond(shared[0] > 0, with_far, own_only, doubled)
    is_right = 1 - seq_index % 2
    own = lax.dynamic_slice_in_dim(pair, is_right * tp_size, tp_size, 0)
    swaps = [(left, left + 1) for left in range(0, seq_size, 2)]
    near = lax.ppermute(own, "seq", swaps + [(right, left) for left, right in swaps])
    out = jax.ShapeDtypeStruct((row_count, lanes), BF16)
    heads = lanes // HEAD_DIM
    square = pltpu.VMEM((heads, WINDOW * TILE, WINDOW * TILE), BF16)
    params = pltpu.CompilerParams(vmem_limit_bytes=24 * 1024 * 1024)
    work = heads * 2 * 12 * (WINDOW * TILE) ** 2 * HEAD_DIM
    cost = pl.CostEstimate(flops=work, bytes_accessed=pair.size * 2, transcendentals=heads * 2 * (WINDOW * TILE) ** 2)
    started = pl.pallas_call(
        far_kernel,
        out_shape=[out] * 4,
        in_specs=[smem, smem, vmem],
        out_specs=[vmem] * 4,
        scratch_shapes=[square, square],
        compiler_params=params,
        cost_estimate=cost,
    )(tile_image, pad_count, pair)
    return pl.pallas_call(
        near_kernel,
        out_shape=[out] * 4,
        in_specs=[smem, smem, vmem, vmem] + [anywhere] * 4,
        out_specs=[anywhere] * 4,
        scratch_shapes=[
            pltpu.VMEM((2, 4, TILE, lanes), BF16),
            square,
            square,
            pltpu.SemaphoreType.DMA((2, 4)),
        ],
        input_output_aliases={4 + index: index for index in range(4)},
        compiler_params=params,
    )(tile_image, pad_count, near, pair, *started)


def solution(mesh):
    rows = P(("seq", "tp"), None)
    out = P("seq", "tp")
    return jax.shard_map(
        body, mesh=mesh, in_specs=(rows,) * 4 + (P(), P()), out_specs=(out,) * 4, check_vma=False
    )
```

time: 103 us -> 101 us (0.981)
  the two profiles are of different devices: /device:TPU:39 before, /device:TPU:7 now
where the time goes in v5:
time: 101 us
  blocking collectives  53.6 us (53%)
  starting transfers between devices  37.9 us (38%)
  Pallas kernels  7.46 us (7%)
  between operations  1.37 us (1%)
    all_to_all x1, blocking collectives, own_only(): lax.all_to_all(chunks[:tp_size], 'tp', split_axis=0, concat_axis=0, tiled...  53.6 us
    ppermute x1, starting transfers between devices, body(): lax.ppermute(own, 'seq', swaps + [(right, left) for left, right in swaps])  37.9 us
    pallas_call x1, Pallas kernels, body(): pl.pallas_call(far_kernel, out_shape=[out] * 4, in_specs=[smem, smem, vme...  5.41 us
  transfers between devices with their start and end apart: 1, of which 0 were waited for; matrix products, arithmetic and copies ran while one was open for 0% of the time, Pallas kernels for 5%

profile of v5, /device:TPU:7, one launch (start us, length us, event | category | flops | bytes accessed | tf_op | source)
XLA Modules:
  0.0 100.8 jit_solution(7417521732839507519)
XLA Ops:
  0.6 1.4 %shard_map.93 = (bf16[16,4,32,384]{3,2,1,0:T(8,128)(2,1)S(1)}, s32[1]{0:T(128)}) custom-call(s32[128]{0:T(128)} %tile_image_ref.5, bf16[32,3072]{1,0:T(8,128)(2,1)} %queries_ref.1, bf16[32,3072]{1,0:T(8,128)(2,1)} %keys_ref.1, bf16[32,3072]{1,0:T(8,128)(2,1)} %values_ref.1, bf16[32,3072]{1,0:T(8,128)(2,1)} %grads_ref.1), custom_call_target="tpu_custom_call" | custom-call | tf_op jit(solution)/shard_map/pallas_call | solution.py:259
  2.7 53.9 %conditional.1 = (bf16[16,4,32,384]{3,2,1,0:T(8,128)(2,1)S(1)}) conditional(s32[]{:T(128)} %bitcast, bf16[16,4,32,384]{3,2,1,0:T(8,128)(2,1)S(1)} %get-tuple-element.16, bf16[16,4,32,384]{3,2,1,0:T(8,128)(2,1)S(1)} %get-tuple-element.16), branch_computations={%region_0.0_spmd, %region_1.0_spmd} | conditional | flops 786432 | bytes 5505032 | solution.py:290
  2.7 0.1 slice.2
  2.8 53.6 %all_to_all.8 = bf16[8,4,32,384]{3,2,1,0:T(8,128)(2,1)S(1)} all-to-all(bf16[8,4,32,384]{3,2,1,0:T(8,128)(2,1)S(1)} %slice.2), channel_id=1, replica_groups=mesh['seq'=64,'tp'=8] {'tp'}, dimensions={0} | all-to-all | bytes 1572864 | tf_op jit(solution)/shard_map/cond/branch_0_fun/all_to_all | solution.py:287
  56.5 0.2 pad_maximum_fusion
  56.6 0.0 copy-start
  56.7 0.0 copy-start.1
  56.7 0.1 constant_dynamic-slice_fusion
  56.8 37.9 %collective-permute-start = (bf16[8,4,32,384]{3,2,1,0:T(8,128)(2,1)S(1)}, bf16[8,4,32,384]{3,2,1,0:T(8,128)(2,1)S(1)}, u32[]{:S(2)}, u32[]{:S(2)}) collective-permute-start(bf16[8,4,32,384]{3,2,1,0:T(8,128)(2,1)S(1)} %constant_dynamic-slice_fusion), channel_id=1, source_target_pairs={{0,8},{16,24},{32,40},{48,56},{64,72},{80,88},{96,104},{112,120},{... | collective-permute-start | bytes 2359304 | tf_op jit(solution)/shard_map/ppermute | solution.py:294
  94.7 0.0 copy-done
  94.7 0.0 copy-done.1
  94.7 5.4 %shard_map.94 = (bf16[256,384]{1,0:T(8,128)(2,1)}, bf16[256,384]{1,0:T(8,128)(2,1)}, bf16[256,384]{1,0:T(8,128)(2,1)}, bf16[256,384]{1,0:T(8,128)(2,1)}) custom-call(s32[128]{0:T(128)S(1)} %copy-done, s32[64]{0:T(128)S(1)} %copy-done.1, bf16[16,4,32,384]{3,2,1,0:T(8,128)(2,1)S(1)} %get-tuple-element.21.pair_ref), custom_call_target="tpu_custom_call" | custom-call | flops 1358954496 | bytes 1572864 | tf_op jit(solution)/shard_map/pallas_call | solution.py:301
  100.1 0.0 collective-permute-done.near_ref
  100.1 0.7 shard_map.95
Async XLA Ops:
  56.6 38.0 %copy-start = (s32[128]{0:T(128)S(1)}, s32[128]{0:T(128)}, u32[]{:S(2)}) copy-start(s32[128]{0:T(128)} %tile_image_ref.5) | copy-start | bytes 1540
  56.7 38.0 %copy-start.1 = (s32[64]{0:T(128)S(1)}, s32[64]{0:T(128)}, u32[]{:S(2)}) copy-start(s32[64]{0:T(128)} %pad_count_ref.3) | copy-start | bytes 772
  56.8 43.3 %collective-permute-start = (bf16[8,4,32,384]{3,2,1,0:T(8,128)(2,1)S(1)}, bf16[8,4,32,384]{3,2,1,0:T(8,128)(2,1)S(1)}, u32[]{:S(2)}, u32[]{:S(2)}) collective-permute-start(bf16[8,4,32,384]{3,2,1,0:T(8,128)(2,1)S(1)} %constant_dynamic-slice_fusion), channel_id=1, source_target_pairs={{0,8},{16,24},{32,40},{48,56},{64,72},{80,88},{96,104},{112,120},{... | collective-permute-start | bytes 2359304 | tf_op jit(solution)/shard_map/ppermute | solution.py:294

commit v6 on v5

--- a/solution.py
+++ b/solution.py
@@ -11,6 +11,14 @@
 LOG2_E = 1.4426950408889634
 BF16 = jnp.bfloat16
 F32 = jnp.float32
+
+
+def group_order(count):
+    return [place for step in range(count) for place in (step, 2 * count - 1 - step)]
+
+
+def chunk_place(token_chunk, count):
+    return jnp.where(token_chunk < count, 2 * token_chunk, 4 * count - 1 - 2 * token_chunk)
 
 
 def pack_kernel(
@@ -47,8 +55,8 @@
     tell.start()
     for index, load in enumerate(loads):
         load.wait()
-        for place in range(2 * count):
-            block = rows.at[index, :, pl.ds(place % count * lanes, lanes)]
+        for place, member in enumerate(group_order(count)):
+            block = rows.at[index, :, pl.ds(member % count * lanes, lanes)]
             pltpu.make_async_copy(block, packed_ref.at[place, index], out_sem).start()
     pltpu.make_async_copy(packed_ref, packed_ref, out_sem).wait()
     tell.wait()
@@ -70,37 +78,35 @@
     return lax.dot_general(left, right, dims, preferred_element_type=F32)
 
 
-def attend(heads, load, first_live, live, weight_buf, grad_buf, stores):
+def attend(load, live, weight_bufs, grad_bufs, stores):
+    heads = len(weight_bufs)
     scaling = HEAD_DIM ** (-0.5)
     contract_last = (((1,), (1,)), ((), ()))
     contract_first = (((0,), (0,)), ((), ()))
     key_row = lax.broadcasted_iota(jnp.int32, (WINDOW * TILE, TILE), 0)
     query_lane = lax.broadcasted_iota(jnp.int32, (1, TILE), 1)
 
-    def inside(places):
-        return (places >= first_live) & (places < first_live + live)
-
     def weigh(head):
         queries, keys, values, grads = load(head)
         for step in range(WINDOW):
             across = slice(step * TILE, (step + 1) * TILE)
-            scores = jnp.where(inside(key_row), dot(keys, queries[across], contract_last), -1e30)
+            scores = jnp.where(key_row < live, dot(keys, queries[across], contract_last), -1e30)
             value_score = dot(values, grads[across], contract_last)
             top = jnp.max(scores, axis=0, keepdims=True)
             raised = jnp.exp2((scores - top) * (scaling * LOG2_E))
             total = jnp.sum(raised, axis=0, keepdims=True)
-            weights = raised * jnp.where(inside(query_lane + step * TILE), 1.0 / total, 0.0)
+            weights = raised * jnp.where(query_lane + step * TILE < live, 1.0 / total, 0.0)
             grad_dot = jnp.sum(weights * value_score, axis=0, keepdims=True)
-            weight_buf[head, :, across] = weights.astype(BF16)
-            grad_buf[head, :, across] = (weights * (value_score - grad_dot)).astype(BF16)
+            weight_bufs[head][:, across] = weights.astype(BF16)
+            grad_bufs[head][:, across] = (weights * (value_score - grad_dot)).astype(BF16)
 
     def collect(head, at, store):
         queries, keys, values, grads = load(head)
         own = pl.ds(pl.multiple_of(at * TILE, TILE), TILE)
-        attended = dot(weight_buf[head, :, own], values, contract_first)
-        query_sum = dot(grad_buf[head, :, own], keys, contract_first)
-        key_sum = jnp.dot(grad_buf[head, own, :], queries, preferred_element_type=F32)
-        value_sum = jnp.dot(weight_buf[head, own, :], grads, preferred_element_type=F32)
+        attended = dot(weight_bufs[head][:, own], values, contract_first)
+        query_sum = dot(grad_bufs[head][:, own], keys, contract_first)
+        key_sum = jnp.dot(grad_bufs[head][own, :], queries, preferred_element_type=F32)
+        value_sum = jnp.dot(weight_bufs[head][own, :], grads, preferred_element_type=F32)
         results = (attended, query_sum * scaling, key_sum * scaling, value_sum)
         store(head, [result.astype(BF16) for result in results])
 
@@ -134,36 +140,45 @@
     return (beyond >= 0) & (beyond <= last) & same
 
 
+def window_load(window):
+    def load(head):
+        lanes = head_lanes(head)
+        return [window[:, index, :, lanes].reshape(WINDOW * TILE, HEAD_DIM) for index in range(4)]
+
+    return load
+
+
 def far_kernel(
-    tile_image_ref, pad_count_ref, pair_ref, attended_ref, query_ref, key_ref, value_ref, weight_buf, grad_buf
+    tile_image_ref, pad_count_ref, pair_ref, attended_ref, query_ref, key_ref, value_ref, window, *bufs
 ):
-    heads = attended_ref.shape[1] // HEAD_DIM
     tile_count = attended_ref.shape[0] // TILE
     per_tile = TILE // pair_ref.shape[2]
+    count = pair_ref.shape[0] // 2
+    heads = len(bufs) // 2
     seq_index = lax.axis_index("seq")
     is_right = 1 - lax.rem(seq_index, 2)
     first_tile = seq_index * tile_count
     near_image = tile_image_ref[first_tile + near_tile(is_right)[0]]
     spans = spans_near(tile_image_ref, first_tile, is_right)
     outs = (attended_ref, query_ref, key_ref, value_ref)
+    mine = [
+        jnp.logical_not(spans & (tile_image_ref[first_tile + tile] == near_image)) for tile in range(tile_count)
+    ]
+    spots = [image_window(tile_image_ref, pad_count_ref, first_tile + tile) for tile in range(tile_count)]
     for tile in range(tile_count):
-        back, live = image_window(tile_image_ref, pad_count_ref, first_tile + tile)
-        place = tile_count * is_right + tile
-        start = jnp.minimum(place - back, 1)
-
-        def load(head):
-            slab = pl.ds(start * per_tile, WINDOW * per_tile)
-            lanes = head_lanes(head)
-            return [pair_ref[slab, index, :, lanes].reshape(WINDOW * TILE, HEAD_DIM) for index in range(4)]
+        start = tile_count * is_right + tile - spots[tile][0]
 
         def store(head, results):
             for out, result in zip(outs, results):
                 out[tile * TILE : (tile + 1) * TILE, head_lanes(head)] = result
 
-        @pl.when(jnp.logical_not(spans & (tile_image_ref[first_tile + tile] == near_image)))
+        @pl.when(mine[tile])
         def _():
-            first_live = (place - back - start) * TILE
-            attend(heads, load, first_live, live, weight_buf, grad_buf, [(place - start, store)])
+            for step in range(WINDOW):
+                within = lax.rem(start + step, 2 * tile_count) * per_tile
+                for chunk in range(per_tile):
+                    window[step * per_tile + chunk] = pair_ref[chunk_place(within + chunk, count)]
+            attend(window_load(window), spots[tile][1], bufs[:heads], bufs[heads:], [(spots[tile][0], store)])
 
 
 def near_kernel(
@@ -180,14 +195,15 @@
     key_ref,
     value_ref,
     results,
-    weight_buf,
-    grad_buf,
+    window,
     sems,
+    *bufs,
 ):
     del attended_in, query_in, key_in, value_in
-    heads = attended_ref.shape[1] // HEAD_DIM
     tile_count = attended_ref.shape[0] // TILE
     per_tile = TILE // pair_ref.shape[2]
+    count = near_ref.shape[0]
+    heads = len(bufs) // 2
     seq_index = lax.axis_index("seq")
     is_right = 1 - lax.rem(seq_index, 2)
     first_tile = seq_index * tile_count
@@ -199,21 +215,19 @@
     start = place - back
     both = tile_image_ref[first_tile] == tile_image_ref[first_tile + 1]
 
-    def load(head):
-        parts = []
-        for index in range(4):
-            tiles = []
-            for step in range(WINDOW):
-                lower = start + step < tile_count
-                from_near = lower == (is_right == 0)
-                within = lax.rem(start + step, tile_count)
-                near_slab = pl.ds(within * per_tile, per_tile)
-                own_slab = pl.ds((within + tile_count * is_right) * per_tile, per_tile)
-                lanes = head_lanes(head)
-                tile = jnp.where(from_near, near_ref[near_slab, index, :, lanes], pair_ref[own_slab, index, :, lanes])
-                tiles.append(tile.reshape(TILE, HEAD_DIM))
-            parts.append(jnp.concatenate(tiles))
-        return parts
+    def gather():
+        for step in range(WINDOW):
+            lower = start + step < tile_count
+            from_near = lower == (is_right == 0)
+            within = lax.rem(start + step, tile_count) * per_tile
+            near_at = [jnp.where(is_right == 1, within + chunk, count - 1 - within - chunk) for chunk in range(per_tile)]
+            own_at = [chunk_place(within + chunk + count * is_right, count) for chunk in range(per_tile)]
+            for wanted, source, places in ((from_near, near_ref, near_at), (~from_near, pair_ref, own_at)):
+
+                @pl.when(wanted)
+                def _():
+                    for chunk in range(per_tile):
+                        window[step * per_tile + chunk] = source[places[chunk]]
 
     def store_at(slot):
         def store(head, values):
@@ -232,7 +246,8 @@
     @pl.when(spans_near(tile_image_ref, first_tile, is_right))
     def _():
         stores = [(place - start, store_at(0)), (both, place - start + other - main, store_at(1))]
-        attend(heads, load, 0, live, weight_buf, grad_buf, stores)
+        gather()
+        attend(window_load(window), live, bufs[:heads], bufs[heads:], stores)
         for copy in copies(0, main):
             copy.start()
 
@@ -274,7 +289,7 @@
         ],
     )(tile_image, queries, keys, values, out_grad)
     groups = [
-        [seq % seq_size * tp_size + tp for seq in (left, left + 1) for tp in range(tp_size)]
+        [(left + place // tp_size) % seq_size * tp_size + place % tp_size for place in group_order(tp_size)]
         for left in range(1, seq_size, 2)
     ]
 
@@ -284,17 +299,18 @@
         )
 
     def own_only(chunks):
-        mine = lax.all_to_all(chunks[:tp_size], "tp", split_axis=0, concat_axis=0, tiled=True)
-        return jnp.concatenate([mine, mine])
+        mine = lax.all_to_all(chunks[::2], "tp", split_axis=0, concat_axis=0, tiled=True)
+        return jnp.stack([mine, mine[::-1]], axis=1).reshape(chunks.shape)
 
     pair = lax.cond(shared[0] > 0, with_far, own_only, doubled)
     is_right = 1 - seq_index % 2
-    own = lax.dynamic_slice_in_dim(pair, is_right * tp_size, tp_size, 0)
+    own = jnp.where(is_right == 1, pair[1::2], pair[::2])
     swaps = [(left, left + 1) for left in range(0, seq_size, 2)]
     near = lax.ppermute(own, "seq", swaps + [(right, left) for left, right in swaps])
     out = jax.ShapeDtypeStruct((row_count, lanes), BF16)
     heads = lanes // HEAD_DIM
-    square = pltpu.VMEM((heads, WINDOW * TILE, WINDOW * TILE), BF16)
+    window = pltpu.VMEM((WINDOW * TILE // chunk, 4, chunk, lanes), BF16)
+    squares = [pltpu.VMEM((WINDOW * TILE, WINDOW * TILE), BF16)] * (2 * heads)
     params = pltpu.CompilerParams(vmem_limit_bytes=24 * 1024 * 1024)
     work = heads * 2 * 12 * (WINDOW * TILE) ** 2 * HEAD_DIM
     cost = pl.CostEstimate(flops=work, bytes_accessed=pair.size * 2, transcendentals=heads * 2 * (WINDOW * TILE) ** 2)
@@ -303,7 +319,7 @@
         out_shape=[out] * 4,
         in_specs=[smem, smem, vmem],
         out_specs=[vmem] * 4,
-        scratch_shapes=[square, square],
+        scratch_shapes=[window, *squares],
         compiler_params=params,
         cost_estimate=cost,
     )(tile_image, pad_count, pair)
@@ -314,9 +330,9 @@
         out_specs=[anywhere] * 4,
         scratch_shapes=[
             pltpu.VMEM((2, 4, TILE, lanes), BF16),
-            square,
-            square,
+            window,
             pltpu.SemaphoreType.DMA((2, 4)),
+            *squares,
         ],
         input_output_aliases={4 + index: index for index in range(4)},
         compiler_params=params,

time: 101 us -> 99.8 us (0.988)
  the two profiles are of different devices: /device:TPU:7 before, /device:TPU:21 now
where the time goes in v6:
time: 99.8 us; the launch traced here: 98.1 us
  blocking collectives  86.6 us (87%)
  Pallas kernels  8.14 us (8%)
  starting transfers between devices  1.92 us (2%)
  between operations  1.34 us (1%)
    all_to_all x1, blocking collectives, with_far(): lax.all_to_all(chunks, ('seq', 'tp'), split_axis=0, concat_axis=0, tiled=...  86.6 us
    pallas_call x1, Pallas kernels, body(): pl.pallas_call(near_kernel, out_shape=[out] * 4, in_specs=[smem, smem, vm...  3.37 us
    pallas_call x1, Pallas kernels, body(): pl.pallas_call(far_kernel, out_shape=[out] * 4, in_specs=[smem, smem, vme...  3.36 us
  transfers between devices with their start and end apart: 1, of which 0 were waited for; matrix products, arithmetic and copies ran while one was open for 0% of the time, Pallas kernels for 3%

profile of v6, /device:TPU:21, one launch (start us, length us, event | category | flops | bytes accessed | tf_op | source)
XLA Modules:
  0.0 98.1 jit_solution(2925521879249602556)
XLA Ops:
  0.6 1.4 %shard_map.93 = (bf16[16,4,32,384]{3,2,1,0:T(8,128)(2,1)S(1)}, s32[1]{0:T(128)}) custom-call(s32[128]{0:T(128)} %tile_image_ref.5, bf16[32,3072]{1,0:T(8,128)(2,1)} %queries_ref.1, bf16[32,3072]{1,0:T(8,128)(2,1)} %keys_ref.1, bf16[32,3072]{1,0:T(8,128)(2,1)} %values_ref.1, bf16[32,3072]{1,0:T(8,128)(2,1)} %grads_ref.1), custom_call_target="tpu_custom_call" | custom-call | tf_op jit(solution)/shard_map/pallas_call | solution.py:274
  2.7 86.6 %conditional.1 = (bf16[16,4,32,384]{3,2,1,0:T(8,128)(2,1)S(1)}) conditional(s32[]{:T(128)} %bitcast.3, bf16[16,4,32,384]{3,2,1,0:T(8,128)(2,1)S(1)} %get-tuple-element.22, bf16[16,4,32,384]{3,2,1,0:T(8,128)(2,1)S(1)} %get-tuple-element.22), branch_computations={%region_0.0_spmd, %region_1.0_spmd} | conditional | flops 786432 | bytes 11010056 | solution.py:305
  2.7 86.6 %all_to_all.9 = bf16[16,4,32,384]{3,2,1,0:T(8,128)(2,1)S(1)} all-to-all(bf16[16,4,32,384]{3,2,1,0:T(8,128)(2,1)S(1)} %param.1), channel_id=1, replica_groups={{8,23,9,22,10,21,11,20,12,19,13,18,14,17,15,16},{24,39,25,38,26,37,27,3..., dimensions={0} | all-to-all | bytes 3145728 | tf_op jit(solution)/shard_map/cond/branch_1_fun/all_to_all | solution.py:297
  89.3 0.0 copy-start
  89.3 0.0 copy-start.1
  89.3 0.1 slice_select_fusion
  89.4 1.9 %collective-permute-start = (bf16[8,4,32,384]{3,2,1,0:T(8,128)(2,1)S(1)}, bf16[8,4,32,384]{3,2,1,0:T(8,128)(2,1)S(1)}, u32[]{:S(2)}, u32[]{:S(2)}) collective-permute-start(bf16[8,4,32,384]{3,2,1,0:T(8,128)(2,1)S(1)} %slice_select_fusion), channel_id=1, source_target_pairs={{0,8},{16,24},{32,40},{48,56},{64,72},{80,88},{96,104},{112,120},{... | collective-permute-start | bytes 2359304 | tf_op jit(solution)/shard_map/ppermute | solution.py:309
  91.3 0.0 copy-done
  91.4 0.0 copy-done.1
  91.4 3.4 %shard_map.94 = (bf16[256,384]{1,0:T(8,128)(2,1)}, bf16[256,384]{1,0:T(8,128)(2,1)}, bf16[256,384]{1,0:T(8,128)(2,1)}, bf16[256,384]{1,0:T(8,128)(2,1)}) custom-call(s32[128]{0:T(128)S(1)} %copy-done, s32[64]{0:T(128)S(1)} %copy-done.1, bf16[16,4,32,384]{3,2,1,0:T(8,128)(2,1)S(1)} %get-tuple-element.27.pair_ref), custom_call_target="tpu_custom_call" | custom-call | flops 1358954496 | bytes 1572864 | tf_op jit(solution)/shard_map/pallas_call | solution.py:317
  94.7 0.0 collective-permute-done.near_ref
  94.7 3.4 %shard_map.95 = (bf16[256,384]{1,0:T(8,128)(2,1)}, bf16[256,384]{1,0:T(8,128)(2,1)}, bf16[256,384]{1,0:T(8,128)(2,1)}, bf16[256,384]{1,0:T(8,128)(2,1)}) custom-call(s32[128]{0:T(128)S(1)} %copy-done, s32[64]{0:T(128)S(1)} %copy-done.1, ...), custom_call_target="tpu_custom_call", output_to_operand_aliasing={{0}: (4, {}), {1}: (5, {}), {2}: (6, {}), {3}: (7, {})} | custom-call | tf_op jit(solution)/shard_map/pallas_call | solution.py:326
Async XLA Ops:
  89.3 2.0 %copy-start = (s32[128]{0:T(128)S(1)}, s32[128]{0:T(128)}, u32[]{:S(2)}) copy-start(s32[128]{0:T(128)} %tile_image_ref.5) | copy-start | bytes 1540
  89.3 2.0 %copy-start.1 = (s32[64]{0:T(128)S(1)}, s32[64]{0:T(128)}, u32[]{:S(2)}) copy-start(s32[64]{0:T(128)} %pad_count_ref.3) | copy-start | bytes 772
  89.4 5.3 %collective-permute-start = (bf16[8,4,32,384]{3,2,1,0:T(8,128)(2,1)S(1)}, bf16[8,4,32,384]{3,2,1,0:T(8,128)(2,1)S(1)}, u32[]{:S(2)}, u32[]{:S(2)}) collective-permute-start(bf16[8,4,32,384]{3,2,1,0:T(8,128)(2,1)S(1)} %slice_select_fusion), channel_id=1, source_target_pairs={{0,8},{16,24},{32,40},{48,56},{64,72},{80,88},{96,104},{112,120},{... | collective-permute-start | bytes 2359304 | tf_op jit(solution)/shard_map/ppermute | solution.py:309

commit v7 on v6

--- a/solution.py
+++ b/solution.py
@@ -14,11 +14,11 @@
 
 
 def group_order(count):
-    return [place for step in range(count) for place in (step, 2 * count - 1 - step)]
+    return [place for step in range(count) for place in (step, count + step)]
 
 
 def chunk_place(token_chunk, count):
-    return jnp.where(token_chunk < count, 2 * token_chunk, 4 * count - 1 - 2 * token_chunk)
+    return jnp.where(token_chunk < count, 2 * token_chunk, 2 * (token_chunk - count) + 1)
 
 
 def pack_kernel(
@@ -220,7 +220,7 @@
             lower = start + step < tile_count
             from_near = lower == (is_right == 0)
             within = lax.rem(start + step, tile_count) * per_tile
-            near_at = [jnp.where(is_right == 1, within + chunk, count - 1 - within - chunk) for chunk in range(per_tile)]
+            near_at = [within + chunk for chunk in range(per_tile)]
             own_at = [chunk_place(within + chunk + count * is_right, count) for chunk in range(per_tile)]
             for wanted, source, places in ((from_near, near_ref, near_at), (~from_near, pair_ref, own_at)):
 
@@ -300,7 +300,7 @@
 
     def own_only(chunks):
         mine = lax.all_to_all(chunks[::2], "tp", split_axis=0, concat_axis=0, tiled=True)
-        return jnp.stack([mine, mine[::-1]], axis=1).reshape(chunks.shape)
+        return jnp.stack([mine, mine], axis=1).reshape(chunks.shape)
 
     pair = lax.cond(shared[0] > 0, with_far, own_only, doubled)
     is_right = 1 - seq_index % 2

time: 99.8 us -> 98.2 us (0.984)
  the two profiles are of different devices: /device:TPU:21 before, /device:TPU:39 now
where the time goes in v7:
time: 98.2 us; the launch traced here: 98 us
  blocking collectives  86.5 us (88%)
  Pallas kernels  8.14 us (8%)
  starting transfers between devices  1.92 us (2%)
  between operations  1.34 us (1%)
    all_to_all x1, blocking collectives, with_far(): lax.all_to_all(chunks, ('seq', 'tp'), split_axis=0, concat_axis=0, tiled=...  86.5 us
    pallas_call x1, Pallas kernels, body(): pl.pallas_call(near_kernel, out_shape=[out] * 4, in_specs=[smem, smem, vm...  3.38 us
    pallas_call x1, Pallas kernels, body(): pl.pallas_call(far_kernel, out_shape=[out] * 4, in_specs=[smem, smem, vme...  3.36 us
  transfers between devices with their start and end apart: 1, of which 0 were waited for; matrix products, arithmetic and copies ran while one was open for 0% of the time, Pallas kernels for 3%

profile of v7, /device:TPU:39, one launch (start us, length us, event | category | flops | bytes accessed | tf_op | source)
XLA Modules:
  0.0 98.0 jit_solution(9885889986940200902)
XLA Ops:
  0.6 1.4 %shard_map.93 = (bf16[16,4,32,384]{3,2,1,0:T(8,128)(2,1)S(1)}, s32[1]{0:T(128)}) custom-call(s32[128]{0:T(128)} %tile_image_ref.5, bf16[32,3072]{1,0:T(8,128)(2,1)} %queries_ref.1, bf16[32,3072]{1,0:T(8,128)(2,1)} %keys_ref.1, bf16[32,3072]{1,0:T(8,128)(2,1)} %values_ref.1, bf16[32,3072]{1,0:T(8,128)(2,1)} %grads_ref.1), custom_call_target="tpu_custom_call" | custom-call | tf_op jit(solution)/shard_map/pallas_call | solution.py:274
  2.7 86.5 %conditional.1 = (bf16[16,4,32,384]{3,2,1,0:T(8,128)(2,1)S(1)}) conditional(s32[]{:T(128)} %bitcast.2, bf16[16,4,32,384]{3,2,1,0:T(8,128)(2,1)S(1)} %get-tuple-element.22, bf16[16,4,32,384]{3,2,1,0:T(8,128)(2,1)S(1)} %get-tuple-element.22), branch_computations={%region_0.0_spmd, %region_1.0_spmd} | conditional | flops 786432 | bytes 8650760 | solution.py:305
  2.7 86.5 %all_to_all.9 = bf16[16,4,32,384]{3,2,1,0:T(8,128)(2,1)S(1)} all-to-all(bf16[16,4,32,384]{3,2,1,0:T(8,128)(2,1)S(1)} %param.1), channel_id=1, replica_groups={{8,16,9,17,10,18,11,19,12,20,13,21,14,22,15,23},{24,32,25,33,26,34,27,3..., dimensions={0} | all-to-all | bytes 3145728 | tf_op jit(solution)/shard_map/cond/branch_1_fun/all_to_all | solution.py:297
  89.2 0.0 copy-start
  89.2 0.0 copy-start.1
  89.2 0.1 slice_select_fusion
  89.3 1.9 %collective-permute-start = (bf16[8,4,32,384]{3,2,1,0:T(8,128)(2,1)S(1)}, bf16[8,4,32,384]{3,2,1,0:T(8,128)(2,1)S(1)}, u32[]{:S(2)}, u32[]{:S(2)}) collective-permute-start(bf16[8,4,32,384]{3,2,1,0:T(8,128)(2,1)S(1)} %slice_select_fusion), channel_id=1, source_target_pairs={{0,8},{16,24},{32,40},{48,56},{64,72},{80,88},{96,104},{112,120},{... | collective-permute-start | bytes 2359304 | tf_op jit(solution)/shard_map/ppermute | solution.py:309
  91.2 0.0 copy-done
  91.2 0.0 copy-done.1
  91.3 3.4 %shard_map.94 = (bf16[256,384]{1,0:T(8,128)(2,1)}, bf16[256,384]{1,0:T(8,128)(2,1)}, bf16[256,384]{1,0:T(8,128)(2,1)}, bf16[256,384]{1,0:T(8,128)(2,1)}) custom-call(s32[128]{0:T(128)S(1)} %copy-done, s32[64]{0:T(128)S(1)} %copy-done.1, bf16[16,4,32,384]{3,2,1,0:T(8,128)(2,1)S(1)} %get-tuple-element.27.pair_ref), custom_call_target="tpu_custom_call" | custom-call | flops 1358954496 | bytes 1572864 | tf_op jit(solution)/shard_map/pallas_call | solution.py:317
  94.6 0.0 collective-permute-done.near_ref
  94.6 3.4 %shard_map.95 = (bf16[256,384]{1,0:T(8,128)(2,1)}, bf16[256,384]{1,0:T(8,128)(2,1)}, bf16[256,384]{1,0:T(8,128)(2,1)}, bf16[256,384]{1,0:T(8,128)(2,1)}) custom-call(s32[128]{0:T(128)S(1)} %copy-done, s32[64]{0:T(128)S(1)} %copy-done.1, ...), custom_call_target="tpu_custom_call", output_to_operand_aliasing={{0}: (4, {}), {1}: (5, {}), {2}: (6, {}), {3}: (7, {})} | custom-call | tf_op jit(solution)/shard_map/pallas_call | solution.py:326
Async XLA Ops:
  89.2 2.0 %copy-start = (s32[128]{0:T(128)S(1)}, s32[128]{0:T(128)}, u32[]{:S(2)}) copy-start(s32[128]{0:T(128)} %tile_image_ref.5) | copy-start | bytes 1540
  89.2 2.0 %copy-start.1 = (s32[64]{0:T(128)S(1)}, s32[64]{0:T(128)}, u32[]{:S(2)}) copy-start(s32[64]{0:T(128)} %pad_count_ref.3) | copy-start | bytes 772
  89.3 5.3 %collective-permute-start = (bf16[8,4,32,384]{3,2,1,0:T(8,128)(2,1)S(1)}, bf16[8,4,32,384]{3,2,1,0:T(8,128)(2,1)S(1)}, u32[]{:S(2)}, u32[]{:S(2)}) collective-permute-start(bf16[8,4,32,384]{3,2,1,0:T(8,128)(2,1)S(1)} %slice_select_fusion), channel_id=1, source_target_pairs={{0,8},{16,24},{32,40},{48,56},{64,72},{80,88},{96,104},{112,120},{... | collective-permute-start | bytes 2359304 | tf_op jit(solution)/shard_map/ppermute | solution.py:309
